TPU v7x, 512 devices: a whole 4x4x16 slice. The times are simulated.
512 devices in a mesh: dir: 8 (over y_lo, x), space: 64 (over z, y_hi, core).
Axes of the slice: x: 4, y: 4 (y_hi: 2, y_lo: 2; y = y_hi * 2 + y_lo), z: 16, core: 2. Of those that a mesh axis runs over, the one named last changes fastest.
Arguments:
- logk: float32 [4, 256, 1024], P(None, 'space'), may hold values from -3 to 3
- storage: float32 [4, 256, 1024], P(None, 'space'), may hold values from 0.5 to 4
- head0: float32 [4, 256, 1024], P(None, 'space'), may hold values from -4 to 4
- support: int32 [4, 256, 1024], P(None, 'space'), may hold values from 0 to 2047
- kweight: float32 [4, 256, 1024], P(None, 'space'), may hold values from 0.1 to 1
- fixed: int32 [256, 1024], P('space'), may hold values 0 or 1
- directions: float32 [32, 2048], P('dir'), may hold values from -4 to 4
- wells: int32 [1024], replicated, may hold values from 0 to 1048575
- rates: float32 [1024], replicated, may hold values from -8 to 8
Outputs:
- head: float32 [4, 256, 1024], P(None, 'space')
- sensitivity: float32 [32, 4, 256, 1024], P('dir', None, 'space')
All inputs are finite; a program needn't handle non-finite values. No bound on the sum of `fixed` on one device may be relied on, other than what follows from the above.
Results may differ from a plain program's by a relative error of at most 0.00002.
Values sent between devices are 32-bit elements; how exact they have to be, the bound alone decides.
No kernel may reach another device: no remote copies, remote signals or barrier semaphores. Data moves between devices by JAX's collectives and lax.ppermute only.
A program may use at most 64 MiB of HBM per device.

v0:
```python
import jax
import jax.numpy as jnp
from jax import lax
from jax.sharding import PartitionSpec as P

STEPS = 2


vertical_ratio = 0.3


def with_halo(cells, sides, width):
    for axis, dim in sides:
        count = lax.axis_size(axis)
        ends = count - 1
        head = lax.slice_in_dim(cells, 0, width, axis=dim)
        tail = lax.slice_in_dim(cells, cells.shape[dim] - width, cells.shape[dim], axis=dim)
        cells = jnp.concatenate(
            [
                lax.ppermute(tail, axis, [(i, (i + 1) % count) for i in range(ends)]),
                cells,
                lax.ppermute(head, axis, [((i + 1) % count, i) for i in range(ends)]),
            ],
            axis=dim,
        )
    return cells


def neighbor_sum(tx, ty, tz, padded):
    center = padded[..., 1:-1, 1:-1]
    widths = [(0, 0)] * (center.ndim - 3) + [(1, 1), (0, 0), (0, 0)]
    vertical = jnp.pad(center, widths)
    total = tx[..., 1:, :] * padded[..., 2:, 1:-1] + tx[..., :-1, :] * padded[..., :-2, 1:-1]
    total = total + ty[..., 1:] * padded[..., 1:-1, 2:] + ty[..., :-1] * padded[..., 1:-1, :-2]
    total = (
        total
        + tz[..., 1:, :, :] * vertical[..., 2:, :, :]
        + tz[..., :-1, :, :] * vertical[..., :-2, :, :]
    )
    return total


def pad_last(field):
    widths = [(0, 0)] * (field.ndim - 1) + [(1, 1)]
    return jnp.pad(field, widths)


def base_sweep(current, start, parts):
    tx, ty, tz, den, store, source, hold = parts
    padded = with_halo(current, (("dir", 2), ("space", 1)), 2)
    inner = neighbor_sum(tx, ty, tz, padded[:, 1:-1, 1:-1])
    return (padded, jnp.where(hold, start, (store * start + source + inner) / den))


def tangent_sweep(dcur, dhead, prev, new, faces, tangents, dsum, store, den, hold):
    tx, ty, tz = faces
    dtx, dty, dtz = tangents
    padded = with_halo(dcur, (("space", 2),), 1)
    acc = neighbor_sum(dtx, dty, dtz, pad_last(prev)) - new * dsum
    acc = acc + neighbor_sum(tx, ty, tz, pad_last(padded)) + store * dhead
    return jnp.where(hold, dhead, acc / den)


def local(logk, storage, head0, support, kweight, fixed, directions, wells, rates):
    layers, rows, width = logk.shape
    first = lax.axis_index("space") * rows
    grid_rows = rows * lax.axis_size("space")
    picked = jnp.take(directions, support, axis=1)
    dlk = jnp.sum(picked * kweight[None], axis=1)
    stacked = jnp.concatenate([logk, storage, fixed[None].astype(jnp.float32), dlk], 0)
    stacked = with_halo(stacked, (("space", 1),), 2)
    logk_wide = stacked[:layers]
    store_wide = stacked[layers : 2 * layers][:, 1:-1]
    hold_wide = jnp.broadcast_to(
        stacked[2 * layers : 2 * layers + 1][:, 1:-1] > 0.5, (layers, rows + 2, width)
    )
    dlk_wide = stacked[2 * layers + 1 :]
    face_pos = first - 1 + lax.iota(jnp.int32, rows + 3)
    valid = ((face_pos >= 1) & (face_pos <= grid_rows - 1)).astype(jnp.float32)
    tx_wide = jnp.exp(0.5 * (logk_wide[:, 1:] + logk_wide[:, :-1])) * valid[None, :, None]
    center = logk_wide[:, 1:-1]
    ty_wide = pad_last(jnp.exp(0.5 * (center[:, :, 1:] + center[:, :, :-1])))
    tz_wide = vertical_ratio * jnp.pad(
        jnp.exp(0.5 * (center[1:] + center[:-1])), ((1, 1), (0, 0), (0, 0))
    )
    den_wide = (
        store_wide
        + tx_wide[:, 1:]
        + tx_wide[:, :-1]
        + ty_wide[:, :, 1:]
        + ty_wide[:, :, :-1]
        + tz_wide[1:]
        + tz_wide[:-1]
    )
    plane = grid_rows * width
    layer = wells // plane
    rest = wells % plane
    local_row = rest // width - (first - 1)
    inside = (local_row >= 0) & (local_row < rows + 2)
    source_wide = (
        jnp.zeros((layers, rows + 2, width), jnp.float32)
        .at[layer, jnp.clip(local_row, 0, rows + 1), rest % width]
        .add(jnp.where(inside, rates, 0.0))
    )
    dlk_mid = dlk_wide[:, 1:-1]
    dtx_wide = tx_wide[None] * (0.5 * (dlk_wide[:, 1:] + dlk_wide[:, :-1]))[:, None]
    side = pad_last(dlk_mid)
    dty_wide = ty_wide[None] * (0.5 * (side[..., 1:] + side[..., :-1]))[:, None]
    dtz_wide = tz_wide[None] * dlk_mid[:, None]
    dsum_wide = (
        dtx_wide[..., 1:, :]
        + dtx_wide[..., :-1, :]
        + dty_wide[..., 1:]
        + dty_wide[..., :-1]
        + dtz_wide[:, 1:]
        + dtz_wide[:, :-1]
    )
    tx = tx_wide[:, 1:-1]
    ty = ty_wide[:, 1:-1]
    tz = tz_wide[:, 1:-1]
    den = den_wide[:, 1:-1]
    hold = hold_wide[:, 1:-1]
    source = source_wide[:, 1:-1]
    dtx = dtx_wide[:, :, 1:-1]
    dty = dty_wide[:, :, 1:-1]
    dtz = dtz_wide[:, :, 1:-1]
    dsum = dsum_wide[:, :, 1:-1]
    trajectory = []
    span = width // lax.axis_size("dir")
    offset = lax.axis_index("dir") * span

    def cut(field, count):
        return lax.dynamic_slice_in_dim(field, offset, count, field.ndim - 1)

    parts = (
        cut(tx, span),
        cut(ty, span + 1),
        cut(tz, span),
        cut(den, span),
        cut(storage, span),
        cut(source, span),
        cut(hold, span),
    )
    current = cut(head0, span)
    for step in range(STEPS):
        start = current
        padded_one, middle = base_sweep(start, start, parts)
        padded_two, current = base_sweep(middle, start, parts)
        tiles = (
            lax.all_gather(padded_one[:, :, 2:-2], "dir", axis=2, tiled=True),
            lax.all_gather(padded_two[:, 1:-1, 2:-2], "dir", axis=2, tiled=True),
            lax.all_gather(current, "dir", axis=2, tiled=True),
        )
        trajectory.append(tiles)
    head = trajectory[-1][2]
    dhead = jnp.zeros(dlk.shape[:1] + logk.shape, jnp.float32)
    for tiles in trajectory:
        start_rims, middle_rims, final = tiles
        dcur = tangent_sweep(
            dhead,
            dhead,
            start_rims[:, 1:-1],
            middle_rims[:, 1:-1],
            (tx, ty, tz),
            (dtx, dty, dtz),
            dsum,
            storage,
            den,
            hold,
        )
        dcur = tangent_sweep(
            dcur, dhead, middle_rims, final, (tx, ty, tz), (dtx, dty, dtz), dsum, storage, den, hold
        )
        dhead = dcur
    return (head, dhead)


def solution(mesh):
    return jax.shard_map(
        local,
        mesh=mesh,
        in_specs=(
            P(None, "space", None),
            P(None, "space", None),
            P(None, "space", None),
            P(None, "space", None),
            P(None, "space", None),
            P("space", None),
            P("dir", None),
            P(),
            P(),
        ),
        out_specs=(P(None, "space", None), P("dir", None, "space", None)),
        check_vma=False,
    )
```

profile of v0, /device:TPU:390, one launch (start us, length us, event | category | flops | bytes accessed | tf_op | source)
XLA Modules:
  0.0 357.6 jit_solution(10112550996427008968)
XLA Ops:
  0.7 6.3 %collective-permute-start.18 = (f32[4,4,1,1024]{3,2,1,0:T(1,128)S(1)}, f32[4,4,1,1024]{3,2,1,0:T(1,128)S(1)}, u32[]{:S(2)}, u32[]{:S(2)}) collective-permute-start(f32[4,4,1,1024]{3,2,1,0:T(1,128)S(1)} %broadcast.155), channel_id=1, source_target_pairs={{1,0},{2,1},{3,2},{4,3},{5,4},{6,5},{7,6},{8,7},{9,8},{10,9},{11,1... | collective-permute-start | bytes 196616 | tf_op jit(solution)/shard_map/ppermute | solution.py:22
  7.1 1.9 collective-permute-start.19
  9.0 0.9 fusion.61
  9.8 0.9 compare_and_fusion
  10.7 1.1 copy.282
  11.9 54.8 %gather_fusion = f32[16384,4]{1,0:T(8,128)} fusion(f32[4,2048]{0,1:T(8,128)S(1)} %copy.282, s32[16384]{0:T(1024)S(1)} %broadcast_clamp_fusion), kind=kCustom, calls=%fused_computation | custom fusion | bytes 589824 | tf_op jit(solution)/shard_map/jit(_take)/gather | solution.py:68
  66.8 7.4 %multiply_reduce_fusion = f32[4,1024,4]{2,1,0:T(8,128)S(1)} fusion(f32[4,4,1024,4]{3,2,1,0:T(8,128)} %bitcast.14, f32[4,4,1024]{2,1,0:T(4,128)} %param.13, pred[4,4,1024]{2,1,0:T(4,128)(4,1)S(1)} %compare_and_fusion), kind=kLoop, calls=%fused_computation.2 | loop fusion | flops 180224 | bytes 409600 | tf_op jit(solution)/shard_map/reduce_sum | solution.py:69
  74.1 0.6 copy.283
  75.0 1.9 collective-permute-start
  77.0 2.5 collective-permute-start.2
  79.5 3.3 collective-permute-start.3
  83.2 4.0 %collective-permute-done.3 = f32[4,4,2]{2,0,1:T(4,128)S(1)} collective-permute-done((f32[4,4,2]{2,0,1:T(4,128)S(1)}, f32[4,4,2]{2,0,1:T(4,128)S(1)}, u32[]{:S(2)}, u32[]{:S(2)}) %collective-permute-start.3) | collective-permute-done | bytes 160 | tf_op jit(solution)/shard_map/ppermute | solution.py:22
  87.2 6.4 %collective-permute-start.4 = (f32[4,2,132]{2,0,1:T(4,128)S(1)}, f32[4,2,132]{2,0,1:T(4,128)S(1)}, u32[]{:S(2)}, u32[]{:S(2)}) collective-permute-start(f32[4,2,132]{2,0,1:T(4,128)S(1)} %get-tuple-element.84), channel_id=1, source_target_pairs={{1,0},{2,1},{3,2},{4,3},{5,4},{6,5},{7,6},{8,7},{9,8},{10,9},{11,1... | collective-permute-start | bytes 12680 | tf_op jit(solution)/shard_map/ppermute | solution.py:22
  93.7 1.9 collective-permute-start.5
  95.6 6.0 %scatter_custom_fusion = f32[24576]{0:T(1024)S(1)} fusion(s32[1024]{0:T(1024)S(1)} %broadcast_select_fusion, f32[1024]{0:T(1024)S(1)} %and_select_fusion, f32[]{:T(128)} %constant.86.clone.1), kind=kCustom, calls=%fused_computation.134 | custom fusion | flops 1024 | bytes 98308
  101.7 0.6 collective-permute-done.5
  102.3 6.7 %collective-permute-start.1 = (f32[13,2,1024]{2,1,0:T(2,128)S(1)}, f32[13,2,1024]{2,1,0:T(2,128)S(1)}, u32[]{:S(2)}, u32[]{:S(2)}) collective-permute-start(f32[13,2,1024]{2,1,0:T(2,128)S(1)} %get-tuple-element.37), channel_id=1, source_target_pairs={{1,0},{2,1},{3,2},{4,3},{5,4},{6,5},{7,6},{8,7},{9,8},{10,9},{11,1... | collective-permute-start | bytes 319496 | tf_op jit(solution)/shard_map/ppermute | solution.py:22
  109.1 28.2 %all_gather.21 = f32[4,8,1024]{2,1,0:T(8,128)S(1)} all-gather(f32[4,8,128]{2,1,0:T(8,128)S(1)} %pad_maximum_fusion.12), channel_id=1, replica_groups=mesh['dir'=8,'space'=64] {'dir'}, dimensions={2}, use_global_device_ids=true | all-gather | bytes 147456 | tf_op jit(solution)/shard_map/all_gather | solution.py:150
  137.3 0.1 pad_slice_fusion.15
  137.5 0.5 select_maximum_fusion.6
  138.1 0.1 pad_maximum_fusion
  138.4 0.2 fusion.49
  138.8 0.1 fusion.53
  139.9 1.9 collective-permute-start.6
  141.8 3.9 %collective-permute-start.7 = (f32[4,4,2]{2,0,1:T(4,128)S(1)}, f32[4,4,2]{2,0,1:T(4,128)S(1)}, u32[]{:S(2)}, u32[]{:S(2)}) collective-permute-start(f32[4,4,2]{2,0,1:T(4,128)S(1)} %get-tuple-element.90), channel_id=1, source_target_pairs={{64,0},{128,64},{192,128},{256,192},{320,256},{384,320},{448,384},... | collective-permute-start | bytes 392 | tf_op jit(solution)/shard_map/ppermute | solution.py:22
  146.0 0.2 fusion.46
  146.3 0.1 fusion.127
  146.5 0.3 fusion.125
  146.8 2.6 collective-permute-done.7
  149.5 1.9 collective-permute-start.8
  151.5 2.4 collective-permute-start.9
  154.4 5.7 %collective-permute-done.9 = f32[4,2,132]{2,0,1:T(4,128)S(1)} collective-permute-done((f32[4,2,132]{2,0,1:T(4,128)S(1)}, f32[4,2,132]{2,0,1:T(4,128)S(1)}, u32[]{:S(2)}, u32[]{:S(2)}) %collective-permute-start.9) | collective-permute-done | bytes 4256 | tf_op jit(solution)/shard_map/ppermute | solution.py:20
  160.2 1.9 collective-permute-start.10
  162.2 3.9 %collective-permute-start.11 = (f32[4,4,2]{2,0,1:T(4,128)S(1)}, f32[4,4,2]{2,0,1:T(4,128)S(1)}, u32[]{:S(2)}, u32[]{:S(2)}) collective-permute-start(f32[4,4,2]{2,0,1:T(4,128)S(1)} %get-tuple-element.88), channel_id=1, source_target_pairs={{64,0},{128,64},{192,128},{256,192},{320,256},{384,320},{448,384},... | collective-permute-start | bytes 392 | tf_op jit(solution)/shard_map/ppermute | solution.py:22
  166.2 28.2 %all_gather.19 = f32[4,6,1024]{2,1,0:T(8,128)S(1)} all-gather(f32[4,6,128]{2,1,0:T(8,128)S(1)} %pad_maximum_fusion.14), channel_id=1, replica_groups=mesh['dir'=8,'space'=64] {'dir'}, dimensions={2}, use_global_device_ids=true | all-gather | bytes 110592 | tf_op jit(solution)/shard_map/all_gather | solution.py:151
  194.4 0.1 fusion.139
  194.5 1.3 divide_select_fusion.2
  196.0 1.9 collective-permute-start.13
  197.9 7.3 %collective-permute-start.12 = (f32[4,2,132]{2,0,1:T(4,128)S(1)}, f32[4,2,132]{2,0,1:T(4,128)S(1)}, u32[]{:S(2)}, u32[]{:S(2)}) collective-permute-start(f32[4,2,132]{2,0,1:T(4,128)S(1)} %get-tuple-element.80), channel_id=1, source_target_pairs={{1,0},{2,1},{3,2},{4,3},{5,4},{6,5},{7,6},{8,7},{9,8},{10,9},{11,1... | collective-permute-start | bytes 12680 | tf_op jit(solution)/shard_map/ppermute | solution.py:22
  205.2 22.1 %all_gather.20 = f32[4,4,1024]{2,0,1:T(4,128)S(1)} all-gather(f32[4,4,128]{2,0,1:T(4,128)S(1)} %fusion.118), channel_id=1, replica_groups=mesh['dir'=8,'space'=64] {'dir'}, dimensions={2}, use_global_device_ids=true | all-gather | bytes 73728 | tf_op jit(solution)/shard_map/all_gather | solution.py:152
  227.3 1.9 collective-permute-start.20
  229.2 2.4 collective-permute-start.21
  231.8 28.2 %all_gather.23 = f32[4,8,1024]{2,1,0:T(8,128)S(1)} all-gather(f32[4,8,128]{2,1,0:T(8,128)S(1)} %pad_maximum_fusion.8), channel_id=1, replica_groups=mesh['dir'=8,'space'=64] {'dir'}, dimensions={2}, use_global_device_ids=true | all-gather | bytes 147456 | tf_op jit(solution)/shard_map/all_gather | solution.py:150
  260.3 5.6 %collective-permute-start.14 = (f32[4,4,2]{2,0,1:T(4,128)S(1)}, f32[4,4,2]{2,0,1:T(4,128)S(1)}, u32[]{:S(2)}, u32[]{:S(2)}) collective-permute-start(f32[4,4,2]{2,0,1:T(4,128)S(1)} %get-tuple-element.87), channel_id=1, source_target_pairs={{0,64},{64,128},{128,192},{192,256},{256,320},{320,384},{384,448},... | collective-permute-start | bytes 392 | tf_op jit(solution)/shard_map/ppermute | solution.py:20
  265.9 1.9 collective-permute-start.15
  267.8 5.7 %collective-permute-done.15 = f32[4,4,2]{2,0,1:T(4,128)S(1)} collective-permute-done((f32[4,4,2]{2,0,1:T(4,128)S(1)}, f32[4,4,2]{2,0,1:T(4,128)S(1)}, u32[]{:S(2)}, u32[]{:S(2)}) %collective-permute-start.15) | collective-permute-done | bytes 160 | tf_op jit(solution)/shard_map/ppermute | solution.py:22
  273.6 1.9 collective-permute-start.17
  275.5 7.3 %collective-permute-start.16 = (f32[4,2,132]{2,0,1:T(4,128)S(1)}, f32[4,2,132]{2,0,1:T(4,128)S(1)}, u32[]{:S(2)}, u32[]{:S(2)}) collective-permute-start(f32[4,2,132]{2,0,1:T(4,128)S(1)} %get-tuple-element.78), channel_id=1, source_target_pairs={{1,0},{2,1},{3,2},{4,3},{5,4},{6,5},{7,6},{8,7},{9,8},{10,9},{11,1... | collective-permute-start | bytes 12680 | tf_op jit(solution)/shard_map/ppermute | solution.py:22
  282.8 0.1 pad_slice_fusion.11
  283.0 1.2 collective-permute-done.16
  284.2 28.3 %all_gather.22 = f32[4,6,1024]{2,1,0:T(8,128)S(1)} all-gather(f32[4,6,128]{2,1,0:T(8,128)S(1)} %pad_maximum_fusion.10), channel_id=1, replica_groups=mesh['dir'=8,'space'=64] {'dir'}, dimensions={2}, use_global_device_ids=true | all-gather | bytes 110592 | tf_op jit(solution)/shard_map/all_gather | solution.py:151
  312.6 0.1 fusion.137
  312.7 0.5 select_maximum_fusion.4
  313.3 1.1 fusion.45
  314.5 1.9 collective-permute-start.22
  316.5 2.4 collective-permute-start.23
  319.0 22.1 %all_gather.18 = f32[4,4,1024]{2,0,1:T(4,128)S(1)} all-gather(f32[4,4,128]{2,0,1:T(4,128)S(1)} %fusion.117), channel_id=1, replica_groups=mesh['dir'=8,'space'=64] {'dir'}, dimensions={2}, use_global_device_ids=true | all-gather | bytes 73728 | tf_op jit(solution)/shard_map/all_gather | solution.py:152
  341.2 0.5 select_maximum_fusion.2
  341.8 1.2 divide_select_fusion.1
  343.0 2.9 collective-permute-start.24
  346.0 1.9 collective-permute-start.25
  348.0 7.2 %collective-permute-done.25 = f32[4,4,1,1024]{3,2,1,0:T(1,128)S(1)} collective-permute-done((f32[4,4,1,1024]{3,2,1,0:T(1,128)S(1)}, f32[4,4,1,1024]{3,2,1,0:T(1,128)S(1)}, u32[]{:S(2)}, u32[]{:S(2)}) %collective-permute-start.25) | collective-permute-done | bytes 65568 | tf_op jit(solution)/shard_map/ppermute | solution.py:20
  355.2 0.5 select_maximum_fusion
  355.7 1.9 divide_select_fusion
  (134 shorter events, 4.6 us)
Async XLA Ops:
  0.6 76.3 %copy-start = (f32[4,4,1024]{2,1,0:T(4,128)S(1)}, f32[4,4,1024]{2,1,0:T(4,128)}, u32[]{:S(2)}) copy-start(f32[4,4,1024]{2,1,0:T(4,128)} %param.11) | copy-start | bytes 196612
  0.6 74.1 %copy-start.4 = (s32[4,1024]{1,0:T(4,128)S(1)}, s32[4,1024]{1,0:T(4,128)}, u32[]{:S(2)}) copy-start(s32[4,1024]{1,0:T(4,128)} %param.14) | copy-start | bytes 49156
  0.7 74.1 %copy-start.1 = (f32[4,4,1024]{2,1,0:T(4,128)S(1)}, f32[4,4,1024]{2,1,0:T(4,128)}, u32[]{:S(2)}) copy-start(f32[4,4,1024]{2,1,0:T(4,128)} %param.10) | copy-start | bytes 196612
  0.7 74.1 %copy-start.2 = (f32[4,4,1024]{2,1,0:T(4,128)S(1)}, f32[4,4,1024]{2,1,0:T(4,128)}, u32[]{:S(2)}) copy-start(f32[4,4,1024]{2,1,0:T(4,128)} %param.9) | copy-start | bytes 196612
  0.7 136.7 %collective-permute-start.18 = (f32[4,4,1,1024]{3,2,1,0:T(1,128)S(1)}, f32[4,4,1,1024]{3,2,1,0:T(1,128)S(1)}, u32[]{:S(2)}, u32[]{:S(2)}) collective-permute-start(f32[4,4,1,1024]{3,2,1,0:T(1,128)S(1)} %broadcast.155), channel_id=1, source_target_pairs={{1,0},{2,1},{3,2},{4,3},{5,4},{6,5},{7,6},{8,7},{9,8},{10,9},{11,1... | collective-permute-start | bytes 196616 | tf_op jit(solution)/shard_map/ppermute | solution.py:22
  7.1 130.4 %collective-permute-start.19 = (f32[4,4,1,1024]{3,2,1,0:T(1,128)S(1)}, f32[4,4,1,1024]{3,2,1,0:T(1,128)S(1)}, u32[]{:S(2)}, u32[]{:S(2)}) collective-permute-start(f32[4,4,1,1024]{3,2,1,0:T(1,128)S(1)} %broadcast.155), channel_id=1, source_target_pairs={{0,1},{1,2},{2,3},{3,4},{4,5},{5,6},{6,7},{7,8},{8,9},{9,10},{10,1... | collective-permute-start | bytes 196616 | tf_op jit(solution)/shard_map/ppermute | solution.py:20
  11.9 71.0 %copy-start.5 = (s32[1024]{0:T(1024)S(1)}, s32[1024]{0:T(1024)}, u32[]{:S(2)}) copy-start(s32[1024]{0:T(1024)} %param.16) | copy-start | bytes 12292
  11.9 71.1 %copy-start.8 = (s32[3]{0:T(128)S(1)}, s32[3]{0:T(128)}, u32[]{:S(2)}) copy-start(s32[3]{0:T(128)} %constant.163) | copy-start | bytes 40
  11.9 71.1 %copy-start.7 = (s32[3]{0:T(128)S(1)}, s32[3]{0:T(128)}, u32[]{:S(2)}) copy-start(s32[3]{0:T(128)} %constant.166) | copy-start | bytes 40
  11.9 71.2 %copy-start.6 = (f32[1024]{0:T(1024)S(1)}, f32[1024]{0:T(1024)}, u32[]{:S(2)}) copy-start(f32[1024]{0:T(1024)} %param.17) | copy-start | bytes 12292
  75.0 63.1 %collective-permute-start = (f32[13,2,1024]{2,1,0:T(2,128)S(1)}, f32[13,2,1024]{2,1,0:T(2,128)S(1)}, u32[]{:S(2)}, u32[]{:S(2)}) collective-permute-start(f32[13,2,1024]{2,1,0:T(2,128)S(1)} %get-tuple-element.36), channel_id=1, source_target_pairs={{0,1},{1,2},{2,3},{3,4},{4,5},{5,6},{6,7},{7,8},{8,9},{9,10},{10,1... | collective-permute-start | bytes 319496 | tf_op jit(solution)/shard_map/ppermute | solution.py:20
  77.0 6.2 %collective-permute-start.2 = (f32[4,4,2]{2,0,1:T(4,128)S(1)}, f32[4,4,2]{2,0,1:T(4,128)S(1)}, u32[]{:S(2)}, u32[]{:S(2)}) collective-permute-start(f32[4,4,2]{2,0,1:T(4,128)S(1)} %get-tuple-element.93), channel_id=1, source_target_pairs={{0,64},{64,128},{128,192},{192,256},{256,320},{320,384},{384,448},... | collective-permute-start | bytes 392 | tf_op jit(solution)/shard_map/ppermute | solution.py:20
  79.5 7.7 %collective-permute-start.3 = (f32[4,4,2]{2,0,1:T(4,128)S(1)}, f32[4,4,2]{2,0,1:T(4,128)S(1)}, u32[]{:S(2)}, u32[]{:S(2)}) collective-permute-start(f32[4,4,2]{2,0,1:T(4,128)S(1)} %get-tuple-element.92), channel_id=1, source_target_pairs={{64,0},{128,64},{192,128},{256,192},{320,256},{384,320},{448,384},... | collective-permute-start | bytes 392 | tf_op jit(solution)/shard_map/ppermute | solution.py:22
  87.2 21.7 %collective-permute-start.4 = (f32[4,2,132]{2,0,1:T(4,128)S(1)}, f32[4,2,132]{2,0,1:T(4,128)S(1)}, u32[]{:S(2)}, u32[]{:S(2)}) collective-permute-start(f32[4,2,132]{2,0,1:T(4,128)S(1)} %get-tuple-element.84), channel_id=1, source_target_pairs={{1,0},{2,1},{3,2},{4,3},{5,4},{6,5},{7,6},{8,7},{9,8},{10,9},{11,1... | collective-permute-start | bytes 12680 | tf_op jit(solution)/shard_map/ppermute | solution.py:22
  93.7 8.6 %collective-permute-start.5 = (f32[4,2,132]{2,0,1:T(4,128)S(1)}, f32[4,2,132]{2,0,1:T(4,128)S(1)}, u32[]{:S(2)}, u32[]{:S(2)}) collective-permute-start(f32[4,2,132]{2,0,1:T(4,128)S(1)} %get-tuple-element.85), channel_id=1, source_target_pairs={{0,1},{1,2},{2,3},{3,4},{4,5},{5,6},{6,7},{7,8},{8,9},{9,10},{10,1... | collective-permute-start | bytes 12680 | tf_op jit(solution)/shard_map/ppermute | solution.py:20
  102.3 35.8 %collective-permute-start.1 = (f32[13,2,1024]{2,1,0:T(2,128)S(1)}, f32[13,2,1024]{2,1,0:T(2,128)S(1)}, u32[]{:S(2)}, u32[]{:S(2)}) collective-permute-start(f32[13,2,1024]{2,1,0:T(2,128)S(1)} %get-tuple-element.37), channel_id=1, source_target_pairs={{1,0},{2,1},{3,2},{4,3},{5,4},{6,5},{7,6},{8,7},{9,8},{10,9},{11,1... | collective-permute-start | bytes 319496 | tf_op jit(solution)/shard_map/ppermute | solution.py:22
  139.9 7.0 %collective-permute-start.6 = (f32[4,4,2]{2,0,1:T(4,128)S(1)}, f32[4,4,2]{2,0,1:T(4,128)S(1)}, u32[]{:S(2)}, u32[]{:S(2)}) collective-permute-start(f32[4,4,2]{2,0,1:T(4,128)S(1)} %get-tuple-element.91), channel_id=1, source_target_pairs={{0,64},{64,128},{128,192},{192,256},{256,320},{320,384},{384,448},... | collective-permute-start | bytes 392 | tf_op jit(solution)/shard_map/ppermute | solution.py:20
  141.8 7.7 %collective-permute-start.7 = (f32[4,4,2]{2,0,1:T(4,128)S(1)}, f32[4,4,2]{2,0,1:T(4,128)S(1)}, u32[]{:S(2)}, u32[]{:S(2)}) collective-permute-start(f32[4,4,2]{2,0,1:T(4,128)S(1)} %get-tuple-element.90), channel_id=1, source_target_pairs={{64,0},{128,64},{192,128},{256,192},{320,256},{384,320},{448,384},... | collective-permute-start | bytes 392 | tf_op jit(solution)/shard_map/ppermute | solution.py:22
  149.5 4.8 %collective-permute-start.8 = (f32[4,2,132]{2,0,1:T(4,128)S(1)}, f32[4,2,132]{2,0,1:T(4,128)S(1)}, u32[]{:S(2)}, u32[]{:S(2)}) collective-permute-start(f32[4,2,132]{2,0,1:T(4,128)S(1)} %get-tuple-element.82), channel_id=1, source_target_pairs={{1,0},{2,1},{3,2},{4,3},{5,4},{6,5},{7,6},{8,7},{9,8},{10,9},{11,1... | collective-permute-start | bytes 12680 | tf_op jit(solution)/shard_map/ppermute | solution.py:22
  151.5 8.6 %collective-permute-start.9 = (f32[4,2,132]{2,0,1:T(4,128)S(1)}, f32[4,2,132]{2,0,1:T(4,128)S(1)}, u32[]{:S(2)}, u32[]{:S(2)}) collective-permute-start(f32[4,2,132]{2,0,1:T(4,128)S(1)} %get-tuple-element.83), channel_id=1, source_target_pairs={{0,1},{1,2},{2,3},{3,4},{4,5},{5,6},{6,7},{7,8},{8,9},{9,10},{10,1... | collective-permute-start | bytes 12680 | tf_op jit(solution)/shard_map/ppermute | solution.py:20
  160.2 35.7 %collective-permute-start.10 = (f32[4,4,2]{2,0,1:T(4,128)S(1)}, f32[4,4,2]{2,0,1:T(4,128)S(1)}, u32[]{:S(2)}, u32[]{:S(2)}) collective-permute-start(f32[4,4,2]{2,0,1:T(4,128)S(1)} %get-tuple-element.89), channel_id=1, source_target_pairs={{0,64},{64,128},{128,192},{192,256},{256,320},{320,384},{384,448},... | collective-permute-start | bytes 392 | tf_op jit(solution)/shard_map/ppermute | solution.py:20
  162.2 33.8 %collective-permute-start.11 = (f32[4,4,2]{2,0,1:T(4,128)S(1)}, f32[4,4,2]{2,0,1:T(4,128)S(1)}, u32[]{:S(2)}, u32[]{:S(2)}) collective-permute-start(f32[4,4,2]{2,0,1:T(4,128)S(1)} %get-tuple-element.88), channel_id=1, source_target_pairs={{64,0},{128,64},{192,128},{256,192},{320,256},{384,320},{448,384},... | collective-permute-start | bytes 392 | tf_op jit(solution)/shard_map/ppermute | solution.py:22
  196.0 35.7 %collective-permute-start.13 = (f32[4,2,132]{2,0,1:T(4,128)S(1)}, f32[4,2,132]{2,0,1:T(4,128)S(1)}, u32[]{:S(2)}, u32[]{:S(2)}) collective-permute-start(f32[4,2,132]{2,0,1:T(4,128)S(1)} %get-tuple-element.81), channel_id=1, source_target_pairs={{0,1},{1,2},{2,3},{3,4},{4,5},{5,6},{6,7},{7,8},{8,9},{9,10},{10,1... | collective-permute-start | bytes 12680 | tf_op jit(solution)/shard_map/ppermute | solution.py:20
  197.9 33.8 %collective-permute-start.12 = (f32[4,2,132]{2,0,1:T(4,128)S(1)}, f32[4,2,132]{2,0,1:T(4,128)S(1)}, u32[]{:S(2)}, u32[]{:S(2)}) collective-permute-start(f32[4,2,132]{2,0,1:T(4,128)S(1)} %get-tuple-element.80), channel_id=1, source_target_pairs={{1,0},{2,1},{3,2},{4,3},{5,4},{6,5},{7,6},{8,7},{9,8},{10,9},{11,1... | collective-permute-start | bytes 12680 | tf_op jit(solution)/shard_map/ppermute | solution.py:22
  227.3 85.4 %collective-permute-start.20 = (f32[4,4,1,1024]{3,2,1,0:T(1,128)S(1)}, f32[4,4,1,1024]{3,2,1,0:T(1,128)S(1)}, u32[]{:S(2)}, u32[]{:S(2)}) collective-permute-start(f32[4,4,1,1024]{3,2,1,0:T(1,128)S(1)} %get-tuple-element.35), channel_id=1, source_target_pairs={{1,0},{2,1},{3,2},{4,3},{5,4},{6,5},{7,6},{8,7},{9,8},{10,9},{11,1... | collective-permute-start | bytes 196616 | tf_op jit(solution)/shard_map/ppermute | solution.py:22
  229.2 83.5 %collective-permute-start.21 = (f32[4,4,1,1024]{3,2,1,0:T(1,128)S(1)}, f32[4,4,1,1024]{3,2,1,0:T(1,128)S(1)}, u32[]{:S(2)}, u32[]{:S(2)}) collective-permute-start(f32[4,4,1,1024]{3,2,1,0:T(1,128)S(1)} %get-tuple-element.34), channel_id=1, source_target_pairs={{0,1},{1,2},{2,3},{3,4},{4,5},{5,6},{6,7},{7,8},{8,9},{9,10},{10,1... | collective-permute-start | bytes 196616 | tf_op jit(solution)/shard_map/ppermute | solution.py:20
  260.3 7.5 %collective-permute-start.14 = (f32[4,4,2]{2,0,1:T(4,128)S(1)}, f32[4,4,2]{2,0,1:T(4,128)S(1)}, u32[]{:S(2)}, u32[]{:S(2)}) collective-permute-start(f32[4,4,2]{2,0,1:T(4,128)S(1)} %get-tuple-element.87), channel_id=1, source_target_pairs={{0,64},{64,128},{128,192},{192,256},{256,320},{320,384},{384,448},... | collective-permute-start | bytes 392 | tf_op jit(solution)/shard_map/ppermute | solution.py:20
  265.9 7.7 %collective-permute-start.15 = (f32[4,4,2]{2,0,1:T(4,128)S(1)}, f32[4,4,2]{2,0,1:T(4,128)S(1)}, u32[]{:S(2)}, u32[]{:S(2)}) collective-permute-start(f32[4,4,2]{2,0,1:T(4,128)S(1)} %get-tuple-element.86), channel_id=1, source_target_pairs={{64,0},{128,64},{192,128},{256,192},{320,256},{384,320},{448,384},... | collective-permute-start | bytes 392 | tf_op jit(solution)/shard_map/ppermute | solution.py:22
  273.6 9.4 %collective-permute-start.17 = (f32[4,2,132]{2,0,1:T(4,128)S(1)}, f32[4,2,132]{2,0,1:T(4,128)S(1)}, u32[]{:S(2)}, u32[]{:S(2)}) collective-permute-start(f32[4,2,132]{2,0,1:T(4,128)S(1)} %get-tuple-element.79), channel_id=1, source_target_pairs={{0,1},{1,2},{2,3},{3,4},{4,5},{5,6},{6,7},{7,8},{8,9},{9,10},{10,1... | collective-permute-start | bytes 12680 | tf_op jit(solution)/shard_map/ppermute | solution.py:20
  275.5 8.6 %collective-permute-start.16 = (f32[4,2,132]{2,0,1:T(4,128)S(1)}, f32[4,2,132]{2,0,1:T(4,128)S(1)}, u32[]{:S(2)}, u32[]{:S(2)}) collective-permute-start(f32[4,2,132]{2,0,1:T(4,128)S(1)} %get-tuple-element.78), channel_id=1, source_target_pairs={{1,0},{2,1},{3,2},{4,3},{5,4},{6,5},{7,6},{8,7},{9,8},{10,9},{11,1... | collective-permute-start | bytes 12680 | tf_op jit(solution)/shard_map/ppermute | solution.py:22
  314.5 26.7 %collective-permute-start.22 = (f32[4,4,1,1024]{3,2,1,0:T(1,128)S(1)}, f32[4,4,1,1024]{3,2,1,0:T(1,128)S(1)}, u32[]{:S(2)}, u32[]{:S(2)}) collective-permute-start(f32[4,4,1,1024]{3,2,1,0:T(1,128)S(1)} %get-tuple-element.33), channel_id=1, source_target_pairs={{1,0},{2,1},{3,2},{4,3},{5,4},{6,5},{7,6},{8,7},{9,8},{10,9},{11,1... | collective-permute-start | bytes 196616 | tf_op jit(solution)/shard_map/ppermute | solution.py:22
  316.5 24.8 %collective-permute-start.23 = (f32[4,4,1,1024]{3,2,1,0:T(1,128)S(1)}, f32[4,4,1,1024]{3,2,1,0:T(1,128)S(1)}, u32[]{:S(2)}, u32[]{:S(2)}) collective-permute-start(f32[4,4,1,1024]{3,2,1,0:T(1,128)S(1)} %get-tuple-element.32), channel_id=1, source_target_pairs={{0,1},{1,2},{2,3},{3,4},{4,5},{5,6},{6,7},{7,8},{8,9},{9,10},{10,1... | collective-permute-start | bytes 196616 | tf_op jit(solution)/shard_map/ppermute | solution.py:20
  341.2 16.4 %copy-start.3 = (f32[4,4,1024]{2,1,0:T(4,128)}, f32[4,4,1024]{2,1,0:T(4,128)S(1)}, u32[]{:S(2)}) copy-start(f32[4,4,1024]{2,1,0:T(4,128)S(1)} %copy.320) | copy-start | bytes 196612
  343.0 4.9 %collective-permute-start.24 = (f32[4,4,1,1024]{3,2,1,0:T(1,128)S(1)}, f32[4,4,1,1024]{3,2,1,0:T(1,128)S(1)}, u32[]{:S(2)}, u32[]{:S(2)}) collective-permute-start(f32[4,4,1,1024]{3,2,1,0:T(1,128)S(1)} %get-tuple-element.31), channel_id=1, source_target_pairs={{1,0},{2,1},{3,2},{4,3},{5,4},{6,5},{7,6},{8,7},{9,8},{10,9},{11,1... | collective-permute-start | bytes 196616 | tf_op jit(solution)/shard_map/ppermute | solution.py:22
  346.0 9.2 %collective-permute-start.25 = (f32[4,4,1,1024]{3,2,1,0:T(1,128)S(1)}, f32[4,4,1,1024]{3,2,1,0:T(1,128)S(1)}, u32[]{:S(2)}, u32[]{:S(2)}) collective-permute-start(f32[4,4,1,1024]{3,2,1,0:T(1,128)S(1)} %get-tuple-element.30), channel_id=1, source_target_pairs={{0,1},{1,2},{2,3},{3,4},{4,5},{5,6},{6,7},{7,8},{8,9},{9,10},{10,1... | collective-permute-start | bytes 196616 | tf_op jit(solution)/shard_map/ppermute | solution.py:20
where the time goes:
time: 359 us; the launch traced here: 358 us
  blocking collectives  157 us (44%)
  starting transfers between devices  86.3 us (24%)
  local copies, waits for them, and re-layouts  60.1 us (17%)
  waiting for transfers between devices  27 us (8%)
  other arithmetic  25.2 us (7%)
    all_gather x2, blocking collectives, local(): lax.all_gather(padded_two[:, 1:-1, 2:-2], 'dir', axis=2, tiled=True)  56.5 us
    all_gather x2, blocking collectives, local(): lax.all_gather(padded_one[:, :, 2:-2], 'dir', axis=2, tiled=True)  56.3 us
    ppermute x13, starting transfers between devices, with_halo(): lax.ppermute(head, axis, [((i + 1) % count, i) for i in range(ends)])  55.7 us
    gather x1, local copies, waits for them, and re-layouts, local(): picked = jnp.take(directions, support, axis=1)  54.8 us
    all_gather x2, blocking collectives, local(): lax.all_gather(current, 'dir', axis=2, tiled=True)  44.3 us
    ppermute x13, starting transfers between devices, with_halo(): lax.ppermute(tail, axis, [(i, (i + 1) % count) for i in range(ends)])  30.6 us
    ppermute x13, waiting for transfers between devices, with_halo(): lax.ppermute(tail, axis, [(i, (i + 1) % count) for i in range(ends)])  13.5 us
    ppermute x13, waiting for transfers between devices, with_halo(): lax.ppermute(head, axis, [((i + 1) % count, i) for i in range(ends)])  13.4 us
  transfers between devices with their start and end apart: 26, of which 7 were waited for; matrix products, arithmetic and copies ran while one was open for 22% of the time, Pallas kernels for 0%

commit v1 on v0

v1 whole, which is shorter than its diff:
```python
import jax
import jax.numpy as jnp
from jax import lax
from jax.experimental import pallas as pl
from jax.experimental.pallas import tpu as pltpu
from jax.sharding import PartitionSpec as P

SUB, LANE = 8, 128
LAYERS, ROWS, DIRS, SUPPORT = 4, 4, 4, 4
WIDE = 3 * ROWS
STEPS, SWEEPS = 2, 2
VERTICAL_RATIO = 0.3

LOGK, HEAD, DLK, STORE, FIXED = 0, 16, 32, 48, 60
PACKED = 63


def row_of(ref, lead, r):
    return ref[lead, pl.ds(r, SUB, stride=ROWS), :]


def gather_pack(logk, head, stor, fixed, supp, kwei, dirs, dlk, fw, bw, table):
    banks = dirs.shape[0] // DIRS
    for k in range(banks * DIRS):
        table[k] = jnp.broadcast_to(dirs[k : k + 1, :], (SUB, LANE))

    def row(r, carry):
        idx = [row_of(supp, s, r) for s in range(SUPPORT)]
        low = [i & (LANE - 1) for i in idx]
        high = [i >> 7 for i in idx]
        acc = [[jnp.zeros((SUB, LANE), jnp.float32) for _ in range(DIRS)] for _ in idx]
        for k in range(banks):
            hit = [h == k for h in high]
            for d in range(DIRS):
                t = table[k * DIRS + d]
                for s in range(SUPPORT):
                    g = jnp.take_along_axis(t, low[s], axis=1, mode="promise_in_bounds")
                    acc[s][d] = jnp.where(hit[s], g, acc[s][d])
        w = [row_of(kwei, s, r) for s in range(SUPPORT)]
        for d in range(DIRS):
            total = acc[0][d] * w[0]
            for s in range(1, SUPPORT):
                total = total + acc[s][d] * w[s]
            dlk[d * ROWS + r] = total
            fw[DLK + d * ROWS + r] = total
            bw[DLK + d * ROWS + r] = total
        return carry

    lax.fori_loop(0, ROWS, row, 0)
    for l in range(LAYERS):
        for r in range(ROWS):
            k = row_of(logk, l, r)
            fw[LOGK + l * ROWS + r] = k
            bw[LOGK + l * ROWS + r] = k
            h = row_of(head, l, r)
            fw[HEAD + l * ROWS + r] = h
            bw[HEAD + l * ROWS + r] = h
            s = row_of(stor, l, r)
            if r > 0:
                fw[STORE + l * 3 + r - 1] = s
            if r < 3:
                bw[STORE + l * 3 + r] = s
    for r in range(ROWS):
        f = fixed[pl.ds(r, SUB, stride=ROWS), :].astype(jnp.float32)
        if r > 0:
            fw[FIXED + r - 1] = f
        if r < 3:
            bw[FIXED + r] = f


def well_source(wells, rates, out):
    first = lax.axis_index("space") * ROWS - 3
    w = wells[...]
    layer = w >> 18
    x = ((w >> 10) & 255) - first
    chunk = (w >> 7) & 7
    inside = (x >= 0) & (x < 10)
    place = jnp.where(inside, (layer * 10 + x) * 8 + chunk, -1)
    count = w.shape[1]
    rows = out.shape[0]
    hit = lax.broadcasted_iota(jnp.int32, (rows, count), 0) == place
    left = jnp.where(hit, jnp.broadcast_to(rates[...], (rows, count)), 0.0)
    lane = lax.broadcasted_iota(jnp.int32, (LANE, count), 0) == (w & (LANE - 1))
    right = lane.astype(jnp.float32)
    out[...] = lax.dot_general(
        left,
        right,
        (((1,), (1,)), ((), ())),
        precision=lax.Precision.HIGHEST,
        preferred_element_type=jnp.float32,
    )


def sweeps_kernel(
    logk, head, stor, fixed, dlk, lft, rgt, src, head_out, sens_out,
    e, g0, g1, g2, g3, txp, txm, typ, tym, tzp, tzm, sc, sw, dl, dlp, dlm, d1, d2, d3,
):
    me = lax.axis_index("space")
    last = lax.axis_size("space") - 1
    keep_left = jnp.where(me > 0, 1.0, 0.0).astype(jnp.float32)
    keep_right = jnp.where(me < last, 1.0, 0.0).astype(jnp.float32)
    lanes = lax.broadcasted_iota(jnp.int32, (SUB, LANE), 1)
    subs = lax.broadcasted_iota(jnp.int32, (SUB, LANE), 0)
    lane_first, lane_last = lanes == 0, lanes == LANE - 1
    y_first = lane_first & (subs == 0)
    y_last = lane_last & (subs == SUB - 1)

    def up(v):
        return pltpu.roll(jnp.where(lane_first, pltpu.roll(v, SUB - 1, 0), v), LANE - 1, 1)

    def down(v):
        return pltpu.roll(jnp.where(lane_last, pltpu.roll(v, 1, 0), v), 1, 1)

    for l in range(LAYERS):
        for r in range(ROWS):
            i = l * ROWS + r
            e[l, r] = jnp.exp(0.5 * lft[LOGK + i])
            e[l, r + 4] = jnp.exp(0.5 * row_of(logk, l, r))
            e[l, r + 8] = jnp.exp(0.5 * rgt[LOGK + i])
            g0[l, r] = lft[HEAD + i]
            g0[l, r + 4] = row_of(head, l, r)
            g0[l, r + 8] = rgt[HEAD + i]
    for d in range(DIRS):
        for r in range(ROWS):
            i = d * ROWS + r
            dl[d, r] = 0.5 * lft[DLK + i]
            dl[d, r + 4] = 0.5 * dlk[i]
            dl[d, r + 8] = 0.5 * rgt[DLK + i]
    for d in range(DIRS):
        for r in range(1, WIDE - 1):
            v = dl[d, r]
            dlp[d, r] = up(v)
            dlm[d, r] = down(v)

    for r in range(1, WIDE - 1):
        if r < 4:
            hold = lft[FIXED + r - 1]
        elif r < 8:
            hold = fixed[pl.ds(r - 4, SUB, stride=ROWS), :].astype(jnp.float32)
        else:
            hold = rgt[FIXED + r - 8]
        held = hold > 0.5
        for l in range(LAYERS):
            if r < 4:
                st = lft[STORE + l * 3 + r - 1]
            elif r < 8:
                st = row_of(stor, l, r - 4)
            else:
                st = rgt[STORE + l * 3 + r - 8]
            c = e[l, r]
            xp, xm = c * e[l, r + 1], c * e[l, r - 1]
            if r == 3:
                xp = xp * keep_left
            if r == 4:
                xm = xm * keep_left
            if r == 7:
                xp = xp * keep_right
            if r == 8:
                xm = xm * keep_right
            yp = jnp.where(y_last, 0.0, c * up(c))
            ym = jnp.where(y_first, 0.0, c * down(c))
            den = st + xp + xm + yp + ym
            if l < LAYERS - 1:
                zp = VERTICAL_RATIO * (c * e[l + 1, r])
                den = den + zp
            if l > 0:
                zm = VERTICAL_RATIO * (c * e[l - 1, r])
                den = den + zm
            inv = 1.0 / den
            w = jnp.where(held, 0.0, inv)
            txp[l, r] = xp * w
            txm[l, r] = xm * w
            typ[l, r] = yp * w
            tym[l, r] = ym * w
            if l < LAYERS - 1:
                tzp[l, r] = zp * w
            if l > 0:
                tzm[l, r] = zm * w
            sc[l, r] = jnp.where(held, 1.0, st * inv)
            sw[l, r] = src[l * 10 + r - 1] * w

    def sweep(count, start, prev, new, dprev, dstart, dnew, r):
        for l in range(LAYERS):
            c = prev[l, r]
            pairs = [
                (txp[l, r], prev[l, r + 1]),
                (txm[l, r], prev[l, r - 1]),
                (typ[l, r], up(c)),
                (tym[l, r], down(c)),
            ]
            if l < LAYERS - 1:
                pairs.append((tzp[l, r], prev[l + 1, r]))
            if l > 0:
                pairs.append((tzm[l, r], prev[l - 1, r]))
            s = sc[l, r]
            value = s * start[l, r] + sw[l, r]
            for t, g in pairs:
                value = value + t * g
            if new is not None:
                new[l, r] = value
            else:
                head_out[l, pl.ds(r - 4, SUB, stride=ROWS), :] = value
            b = [t * (g - value) for t, g in pairs]
            flat = (b[0] + b[1]) + (b[2] + b[3])
            tall = b[4] + b[5] if len(b) == 6 else b[4]
            own = flat + (tall + tall)
            for d in range(DIRS):
                acc = own * dl[d, r] + b[0] * dl[d, r + 1] + b[1] * dl[d, r - 1]
                acc = acc + b[2] * dlp[d, r] + b[3] * dlm[d, r]
                if dprev is not None:
                    v = dprev[d, l, r]
                    acc = acc + pairs[0][0] * dprev[d, l, r + 1] + pairs[1][0] * dprev[d, l, r - 1]
                    acc = acc + pairs[2][0] * up(v) + pairs[3][0] * down(v)
                    n = 4
                    if l < LAYERS - 1:
                        acc = acc + pairs[n][0] * dprev[d, l + 1, r]
                        n += 1
                    if l > 0:
                        acc = acc + pairs[n][0] * dprev[d, l - 1, r]
                if dstart is not None:
                    acc = acc + s * dstart[d, l, r]
                if dnew is not None:
                    dnew[d, l, r] = acc
                else:
                    sens_out[d, l, pl.ds(r - 4, SUB, stride=ROWS), :] = acc

    def run(lo, hi, *what):
        def body(r, carry):
            sweep(0, *what, r)
            return carry

        lax.fori_loop(lo, hi, body, 0)

    run(1, 11, g0, g0, g1, None, None, d1)
    run(2, 10, g0, g1, g2, d1, None, d2)
    run(3, 9, g2, g2, g3, d2, d2, d3)
    for r in range(4, 8):
        sweep(0, g2, g3, None, d3, d2, None, r)


def tiles(x):
    lead, rows, width = x.shape
    x = x.reshape(lead, rows, width // LANE, LANE).transpose(0, 2, 1, 3)
    return x.reshape(lead, rows * width // LANE, LANE)


def rows_back(x, lead):
    x = x.reshape(*lead, SUB, ROWS, LANE)
    x = jnp.swapaxes(x, -3, -2)
    return x.reshape(*lead, ROWS, SUB * LANE)


def local(logk, storage, head0, support, kweight, fixed, directions, wells, rates):
    f32 = jnp.float32
    vmem = pl.BlockSpec(memory_space=pltpu.VMEM)
    logk, storage, head0, support, kweight = map(
        tiles, (logk, storage, head0, support, kweight)
    )
    fixed = tiles(fixed[None])[0]
    table = tiles(directions[None])[0]
    count = lax.axis_size("space")
    pack = jax.ShapeDtypeStruct((PACKED, SUB, LANE), f32)
    dlk, fw, bw = pl.pallas_call(
        gather_pack,
        out_shape=(jax.ShapeDtypeStruct((DIRS * ROWS, SUB, LANE), f32), pack, pack),
        in_specs=[vmem] * 7,
        out_specs=(vmem,) * 3,
        scratch_shapes=[pltpu.VMEM((table.shape[0], SUB, LANE), f32)],
        name="gather_pack",
    )(logk, head0, storage, fixed, support, kweight, table)
    lft = lax.ppermute(fw, "space", [(i, i + 1) for i in range(count - 1)])
    rgt = lax.ppermute(bw, "space", [(i + 1, i) for i in range(count - 1)])
    src = pl.pallas_call(
        well_source,
        out_shape=jax.ShapeDtypeStruct((LAYERS * 10 * SUB, LANE), f32),
        in_specs=[vmem] * 2,
        out_specs=vmem,
        name="well_source",
    )(wells[None], rates[None])
    src = src.reshape(LAYERS * 10, SUB, LANE)
    grid = pltpu.VMEM((LAYERS, WIDE, SUB, LANE), f32)
    field = pltpu.VMEM((DIRS, LAYERS, WIDE, SUB, LANE), f32)
    plane = pltpu.VMEM((DIRS, WIDE, SUB, LANE), f32)
    head, sens = pl.pallas_call(
        sweeps_kernel,
        out_shape=(
            jax.ShapeDtypeStruct((LAYERS, SUB * ROWS, LANE), f32),
            jax.ShapeDtypeStruct((DIRS, LAYERS, SUB * ROWS, LANE), f32),
        ),
        in_specs=[vmem] * 8,
        out_specs=(vmem, vmem),
        scratch_shapes=[grid] * 13 + [plane] * 3 + [field] * 3,
        name="sweeps",
    )(logk, head0, storage, fixed, dlk, lft, rgt, src)
    return rows_back(head, (LAYERS,)), rows_back(sens, (DIRS, LAYERS))


def solution(mesh):
    rows = P(None, "space", None)
    return jax.shard_map(
        local,
        mesh=mesh,
        in_specs=(rows,) * 5 + (P("space", None), P("dir", None), P(), P()),
        out_specs=(rows, P("dir", None, "space", None)),
        check_vma=False,
    )
```

time: 359 us -> 29.5 us (0.08)
  the two profiles are of different devices: /device:TPU:390 before, /device:TPU:255 now
where the time goes in v1:
time: 29.5 us; the launch traced here: 29.3 us
  Pallas kernels  13.2 us (45%)
  starting transfers between devices  7.9 us (27%)
  waiting for transfers between devices  6.81 us (23%)
  local copies, waits for them, and re-layouts  0.69 us (2%)
  between operations  0.65 us (2%)
    ppermute x1, waiting for transfers between devices, local(): rgt = lax.ppermute(bw, 'space', [(i + 1, i) for i in range(count - 1)])  6.8 us
    ppermute x1, starting transfers between devices, local(): lft = lax.ppermute(fw, 'space', [(i, i + 1) for i in range(count - 1)])  5.98 us
    pallas_call x1, Pallas kernels, local(): pl.pallas_call(sweeps_kernel, out_shape=(jax.ShapeDtypeStruct((LAYERS, SU...  5.61 us
    pallas_call x1, Pallas kernels, local(): pl.pallas_call(gather_pack, out_shape=(jax.ShapeDtypeStruct((DIRS * ROWS,...  4.89 us
    pallas_call x1, Pallas kernels, local(): pl.pallas_call(well_source, out_shape=jax.ShapeDtypeStruct((LAYERS * 10 *...  2.73 us
    ppermute x1, starting transfers between devices, local(): rgt = lax.ppermute(bw, 'space', [(i + 1, i) for i in range(count - 1)])  1.92 us
    unnamed x4, local copies, waits for them, and re-layouts  0.69 us
  transfers between devices with their start and end apart: 2, of which 1 were waited for; matrix products, arithmetic and copies ran while one was open for 0% of the time, Pallas kernels for 9%

profile of v1, /device:TPU:255, one launch (start us, length us, event | category | flops | bytes accessed | tf_op | source)
XLA Modules:
  0.0 29.3 jit_solution(13606276062426672042)
XLA Ops:
  0.6 4.9 %gather_pack.1 = (f32[16,8,128]{2,1,0:T(8,128)}, f32[63,8,128]{2,1,0:T(8,128)}, f32[63,8,128]{2,1,0:T(8,128)}) custom-call(f32[4,32,128]{2,1,0:T(8,128)} %bitcast.49, f32[4,32,128]{2,1,0:T(8,128)} %bitcast.51, f32[4,32,128]{2,1,0:T(8,128)} %bitcast.53, s32[32,128]{1,0:T(8,128)} %bitcast.57, s32[4,32,128]{2,1,0:T(8,128)} %bitcast.55, f32[4,32,128]{2,1,0:T(8,128)} %bitcast.56, ...), custom_call_target="tpu_custom_call" | custom-call | tf_op jit(solution)/shard_map/gather_pack/pallas_call | solution.py:263
  5.5 6.0 %collective-permute-start = (f32[63,8,128]{2,1,0:T(8,128)}, f32[63,8,128]{2,1,0:T(8,128)S(1)}, u32[]{:S(2)}, u32[]{:S(2)}) collective-permute-start(f32[63,8,128]{2,1,0:T(8,128)} %get-tuple-element.8), channel_id=1, source_target_pairs={{0,1},{1,2},{2,3},{3,4},{4,5},{5,6},{6,7},{7,8},{8,9},{9,10},{10,1... | collective-permute-start | bytes 774152 | tf_op jit(solution)/shard_map/ppermute | solution.py:271
  11.5 1.9 %collective-permute-start.1 = (f32[63,8,128]{2,1,0:T(8,128)}, f32[63,8,128]{2,1,0:T(8,128)S(1)}, u32[]{:S(2)}, u32[]{:S(2)}) collective-permute-start(f32[63,8,128]{2,1,0:T(8,128)} %get-tuple-element.9), channel_id=1, source_target_pairs={{1,0},{2,1},{3,2},{4,3},{5,4},{6,5},{7,6},{8,7},{9,8},{10,9},{11,1... | collective-permute-start | bytes 774152 | tf_op jit(solution)/shard_map/ppermute | solution.py:272
  13.4 2.7 %well_source.1 = f32[320,128]{1,0:T(8,128)} custom-call(s32[1,1024]{1,0:T(1,128)} %bitcast.60, f32[1,1024]{1,0:T(1,128)} %bitcast.61), custom_call_target="tpu_custom_call" | custom-call | tf_op jit(solution)/shard_map/well_source/pallas_call | solution.py:273
  16.2 0.0 collective-permute-done.lft
  16.2 0.0 copy-start
  16.2 6.8 %collective-permute-done.1.rgt = f32[63,8,128]{2,1,0:T(8,128)S(1)} collective-permute-done((f32[63,8,128]{2,1,0:T(8,128)}, f32[63,8,128]{2,1,0:T(8,128)S(1)}, u32[]{:S(2)}, u32[]{:S(2)}) %collective-permute-start.1) | collective-permute-done | bytes 258080 | tf_op jit(solution)/shard_map/ppermute | solution.py:272
  23.0 0.0 copy-start.1
  23.0 0.0 copy-done
  23.0 0.7 %copy-done.1 = f32[63,8,128]{2,1,0:T(8,128)} copy-done((f32[63,8,128]{2,1,0:T(8,128)}, f32[63,8,128]{2,1,0:T(8,128)S(1)}, u32[]{:S(2)}) %copy-start.1) | copy-done | bytes 258072
  23.7 5.6 %sweeps.1 = (f32[4,32,128]{2,1,0:T(8,128)}, f32[4,4,32,128]{3,2,1,0:T(8,128)}) custom-call(f32[4,32,128]{2,1,0:T(8,128)} %bitcast.50, f32[4,32,128]{2,1,0:T(8,128)} %bitcast.52, f32[4,32,128]{2,1,0:T(8,128)} %bitcast.54, s32[32,128]{1,0:T(8,128)} %bitcast.58, f32[16,8,128]{2,1,0:T(8,128)} %get-tuple-element.7.dlk, f32[63,8,128]{2,1,0:T(8,128)} %copy-done, ...), custom_call_target="tpu_custom_call" | custom-call | tf_op jit(solution)/shard_map/sweeps/pallas_call | solution.py:284
Async XLA Ops:
  5.5 10.6 %collective-permute-start = (f32[63,8,128]{2,1,0:T(8,128)}, f32[63,8,128]{2,1,0:T(8,128)S(1)}, u32[]{:S(2)}, u32[]{:S(2)}) collective-permute-start(f32[63,8,128]{2,1,0:T(8,128)} %get-tuple-element.8), channel_id=1, source_target_pairs={{0,1},{1,2},{2,3},{3,4},{4,5},{5,6},{6,7},{7,8},{8,9},{9,10},{10,1... | collective-permute-start | bytes 774152 | tf_op jit(solution)/shard_map/ppermute | solution.py:271
  11.5 11.5 %collective-permute-start.1 = (f32[63,8,128]{2,1,0:T(8,128)}, f32[63,8,128]{2,1,0:T(8,128)S(1)}, u32[]{:S(2)}, u32[]{:S(2)}) collective-permute-start(f32[63,8,128]{2,1,0:T(8,128)} %get-tuple-element.9), channel_id=1, source_target_pairs={{1,0},{2,1},{3,2},{4,3},{5,4},{6,5},{7,6},{8,7},{9,8},{10,9},{11,1... | collective-permute-start | bytes 774152 | tf_op jit(solution)/shard_map/ppermute | solution.py:272
  16.2 6.8 %copy-start = (f32[63,8,128]{2,1,0:T(8,128)}, f32[63,8,128]{2,1,0:T(8,128)S(1)}, u32[]{:S(2)}) copy-start(f32[63,8,128]{2,1,0:T(8,128)S(1)} %collective-permute-done.lft) | copy-start | bytes 774148
  23.0 0.7 %copy-start.1 = (f32[63,8,128]{2,1,0:T(8,128)}, f32[63,8,128]{2,1,0:T(8,128)S(1)}, u32[]{:S(2)}) copy-start(f32[63,8,128]{2,1,0:T(8,128)S(1)} %collective-permute-done.1.rgt) | copy-start | bytes 774148

commit v2 on v1

v2 whole, which is shorter than its diff:
```python
import jax
import jax.numpy as jnp
from jax import lax
from jax.experimental import pallas as pl
from jax.experimental.pallas import tpu as pltpu
from jax.sharding import PartitionSpec as P

SUB, LANE = 8, 128
LAYERS, ROWS, DIRS, SUPPORT = 4, 4, 4, 4
WIDE = 3 * ROWS
VERTICAL = 0.3
VMEM_BYTES = 16 * 2**20

LOGK, HEAD, DLK, STORE, FIXED, FULL = 0, 16, 32, 48, 64, 68
SENT_FIXED, NEAR, FAR = 60, 63, 64

GRID, PLANE, FIELD = LAYERS * WIDE, DIRS * WIDE, DIRS * LAYERS * WIDE
E, G0, G1, G2, G3, H0, H2, SC, PP, S0, SW = (i * GRID for i in range(11))
DL = 11 * GRID
DLU, DLD = DL + PLANE, DL + 2 * PLANE
KK = DL + 3 * PLANE
D1, D2, D3 = KK + FIELD, KK + 2 * FIELD, KK + 3 * FIELD
STATE = KK + 4 * FIELD


def tile(k):
    if isinstance(k, int):
        return pl.ds(k * SUB, SUB)
    return pl.ds(pl.multiple_of(k * SUB, SUB), SUB)


def odd():
    return lax.rem(lax.axis_index("space"), 2)


def gather_pack(*refs):
    hbm, (own, near, far), vmem, sem = refs[:7], refs[7:10], refs[10:17], refs[17]
    loads = [pltpu.make_async_copy(a, b, sem.at[i]) for i, (a, b) in enumerate(zip(hbm, vmem))]
    for load in loads[::-1]:
        load.start()
    logk, head, stor, fixed, supp, kwei, dirs = vmem
    p = odd()
    for load in loads[4:]:
        load.wait()

    def source_row(j):
        return jnp.where(p == 1, j, 3 - j)

    t = dirs[...]
    t_high = t.astype(jnp.bfloat16)
    t_low = (t - t_high.astype(jnp.float32)).astype(jnp.bfloat16)
    left = jnp.concatenate([t_high, t_low], axis=1)
    banks = dirs.shape[0] // DIRS
    places = lax.broadcasted_iota(jnp.int32, (LANE, LANE), 0).astype(jnp.bfloat16)
    half = lax.broadcasted_iota(jnp.int32, (SUB, LANE), 0) >> 2
    one, zero = jnp.bfloat16(1), jnp.bfloat16(0)

    def block(i, carry):
        j, pair = i >> 2, i & 3
        r = source_row(j)
        total = [None, None]
        for s in range(SUPPORT):
            hot, high, weight = [], [], []
            for h in range(2):
                at = (2 * pair + h) * ROWS + r
                idx = jnp.broadcast_to(supp[s, pl.ds(at, 1), :], (SUB, LANE))
                low = (idx & (LANE - 1)).astype(jnp.float32)
                low = jnp.concatenate([low, low], axis=0).astype(jnp.bfloat16)
                low = jnp.concatenate([low] * (LANE // 16), axis=0)
                hot.append(jnp.where(places == low, one, zero))
                high.append((idx >> 7) - half)
                weight.append(jnp.broadcast_to(kwei[s, pl.ds(at, 1), :], (SUB, LANE)))
            right = jnp.concatenate(hot, axis=1)
            right = jnp.concatenate([right, right], axis=0)
            found = jnp.dot(left, right, preferred_element_type=jnp.float32)
            for h in range(2):
                value = jnp.zeros((SUB, LANE), jnp.float32)
                for m in range(banks // 2):
                    part = found[m * SUB : (m + 1) * SUB, h * LANE : (h + 1) * LANE]
                    value = jnp.where(high[h] == 2 * m, part, value)
                value = value * weight[h]
                total[h] = value if total[h] is None else total[h] + value
        for h in range(2):
            done = (total[h] + pltpu.roll(total[h], 4, 0))[:DIRS]
            at = DLK * SUB + j * SUB + 2 * pair + h
            own[pl.ds(at, DIRS, stride=ROWS * SUB), :] = done
            near[pl.ds(at, DIRS, stride=ROWS * SUB), :] = done
            far[pl.ds(at, DIRS, stride=ROWS * SUB), :] = done
        return carry

    lax.fori_loop(0, 4 * ROWS, block, 0)
    for load in loads[:4]:
        load.wait()
    far[tile(NEAR), :] = jnp.zeros((SUB, LANE), jnp.float32)
    for j in range(ROWS):
        r = source_row(j)
        for l in range(LAYERS):
            rows = pl.ds(r, SUB, stride=ROWS)
            k = logk[l, rows, :]
            own[tile(LOGK + l * ROWS + j), :] = k
            near[tile(LOGK + l * ROWS + j), :] = k
            far[tile(LOGK + l * ROWS + j), :] = k
            h = head[l, rows, :]
            own[tile(HEAD + l * ROWS + j), :] = h
            near[tile(HEAD + l * ROWS + j), :] = h
            far[tile(HEAD + l * ROWS + j), :] = h
            s = stor[l, rows, :]
            own[tile(STORE + l * ROWS + j), :] = s
            if j > 0:
                far[tile(STORE + l * 3 + j - 1), :] = s
            if j < 3:
                near[tile(STORE + l * 3 + j), :] = s
        f = fixed[pl.ds(r, SUB, stride=ROWS), :].astype(jnp.float32)
        own[tile(FIXED + j), :] = f
        if j > 0:
            far[tile(SENT_FIXED + j - 1), :] = f
        if j < 3:
            near[tile(SENT_FIXED + j), :] = f


def well_source(wells_hbm, rates_hbm, out, wells, rates, sem):
    loads = [
        pltpu.make_async_copy(wells_hbm, wells, sem.at[0]),
        pltpu.make_async_copy(rates_hbm, rates, sem.at[1]),
    ]
    for load in loads:
        load.start()
    p = odd()
    for load in loads:
        load.wait()
    first = lax.axis_index("space") * ROWS
    w = wells[...]
    x = ((w >> 10) & 255) - first
    place = jnp.where(p == 1, 3 - x, x) + 3
    inside = (place >= 0) & (place < 10)
    place = jnp.where(inside, ((w >> 18) * 10 + place) * SUB + ((w >> 7) & 7), -1)
    count = w.shape[1]
    rows = out.shape[0]
    hit = lax.broadcasted_iota(jnp.int32, (rows, count), 0) == place
    left = jnp.where(hit, jnp.broadcast_to(rates[...], (rows, count)), 0.0)
    lane = lax.broadcasted_iota(jnp.int32, (LANE, count), 0) == (w & (LANE - 1))
    out[...] = lax.dot_general(
        left,
        lane.astype(jnp.float32),
        (((1,), (1,)), ((), ())),
        precision=lax.Precision.HIGHEST,
        preferred_element_type=jnp.float32,
    )


class Sweeper:
    def __init__(self, st, src):
        self.st, self.src = st, src
        lanes = lax.broadcasted_iota(jnp.int32, (SUB, LANE), 1)
        subs = lax.broadcasted_iota(jnp.int32, (SUB, LANE), 0)
        self.lane_first, self.lane_last = lanes == 0, lanes == LANE - 1
        self.sub_first, self.sub_last = subs == 0, subs == SUB - 1

    def get(self, base, i):
        return self.st[tile(base + i), :]

    def put(self, base, i, v):
        self.st[tile(base + i), :] = v

    def up(self, v):
        edge = jnp.where(self.sub_last, 0.0, pltpu.roll(v, SUB - 1, 0))
        return pltpu.roll(jnp.where(self.lane_first, edge, v), LANE - 1, 1)

    def down(self, v):
        edge = jnp.where(self.sub_first, 0.0, pltpu.roll(v, 1, 0))
        return pltpu.roll(jnp.where(self.lane_last, edge, v), 1, 1)

    def fill(self, pack, place, keep=None):
        for l in range(LAYERS):
            for j in range(ROWS):
                i = l * WIDE + place(j)
                e = jnp.exp(0.5 * pack[tile(LOGK + l * ROWS + j), :])
                if keep is not None:
                    e = e * keep
                h = pack[tile(HEAD + l * ROWS + j), :]
                self.put(E, i, e)
                self.put(G0, i, e * h)
                self.put(H0, i, h)
        for d in range(DIRS):
            for j in range(ROWS):
                i = d * WIDE + place(j)
                v = 0.5 * pack[tile(DLK + d * ROWS + j), :]
                self.put(DL, i, v)
                if 0 < place(j) < WIDE - 1:
                    self.put(DLU, i, self.up(v))
                    self.put(DLD, i, self.down(v))

    def coefficients(self, w, pack, store_at, fixed_at, missing=None):
        held = pack[tile(fixed_at), :] > 0.5
        dl = [[self.get(DL, d * WIDE + w + o) for o in (-1, 0, 1)] for d in range(DIRS)]
        dlu = [self.get(DLU, d * WIDE + w) for d in range(DIRS)]
        dld = [self.get(DLD, d * WIDE + w) for d in range(DIRS)]
        for l in range(LAYERS):
            i = l * WIDE + w
            e = self.get(E, i)
            xp, xm = self.get(E, i + 1), self.get(E, i - 1)
            yp, ym = self.up(e), self.down(e)
            tall = None
            if l < LAYERS - 1:
                tall = self.get(E, i + WIDE)
            if l > 0:
                below = self.get(E, i - WIDE)
                tall = below if tall is None else tall + below
            tall = VERTICAL * tall
            total = ((xp + xm) + (yp + ym)) + tall
            store = pack[tile(store_at(l)), :]
            if missing is not None:
                store = store + missing
            inv = 1.0 / (store + e * total)
            free = jnp.where(held, 0.0, inv)
            self.put(S0, i, total)
            self.put(PP, i, free * e)
            self.put(SC, i, jnp.where(held, 1.0, store * inv))
            self.put(SW, i, self.src[tile(l * 10 + w - 1), :] * free)
            for d in range(DIRS):
                k = xp * dl[d][2] + xm * dl[d][0] + yp * dlu[d] + ym * dld[d] + tall * dl[d][1]
                self.put(KK, (d * LAYERS + l) * WIDE + w, k)

    def sweep(self, number, w, outs=None):
        start = H0 if number < 3 else H2
        prev = (G0, G1, G2, G3)[number - 1]
        new = (G1, G2, G3, None)[number - 1]
        dprev = (None, D1, D2, D3)[number - 1]
        dnew = (D1, D2, D3, None)[number - 1]
        get = self.get
        dl = [[get(DL, d * WIDE + w + o) for o in (-1, 0, 1)] for d in range(DIRS)]
        dlu = [get(DLU, d * WIDE + w) for d in range(DIRS)]
        dld = [get(DLD, d * WIDE + w) for d in range(DIRS)]
        for l in range(LAYERS):
            i = l * WIDE + w
            here = get(prev, i)
            xp, xm = get(prev, i + 1), get(prev, i - 1)
            yp, ym = self.up(here), self.down(here)
            tall = None
            if l < LAYERS - 1:
                tall = get(prev, i + WIDE)
            if l > 0:
                below = get(prev, i - WIDE)
                tall = below if tall is None else tall + below
            tall = VERTICAL * tall
            total = ((xp + xm) + (yp + ym)) + tall
            e, sc, pp = get(E, i), get(SC, i), get(PP, i)
            value = sc * get(start, i) + get(SW, i) + pp * total
            if new is not None:
                self.put(new, i, e * value)
            if number == 2:
                self.put(H2, i, value)
            if outs is not None:
                outs[0][l, outs[2], :] = value
            own = (total - value * get(S0, i)) + tall
            scaled = pp if outs is not None else pp * e
            for d in range(DIRS):
                f = (d * LAYERS + l) * WIDE + w
                acc = own * dl[d][1] - value * get(KK, f)
                acc = acc + (xp * dl[d][2] + xm * dl[d][0])
                acc = acc + (yp * dlu[d] + ym * dld[d])
                if dprev is not None:
                    v = get(dprev, f)
                    acc = acc + (get(dprev, f + 1) + get(dprev, f - 1))
                    acc = acc + (self.up(v) + self.down(v))
                    side = None
                    if l < LAYERS - 1:
                        side = get(dprev, f + WIDE)
                    if l > 0:
                        below = get(dprev, f - WIDE)
                        side = below if side is None else side + below
                    acc = acc + VERTICAL * side
                out = scaled * acc
                if number == 3:
                    out = out + sc * get(D2, f)
                if dnew is not None:
                    self.put(dnew, f, out)
                else:
                    outs[1][d, l, outs[2], :] = out + (sc / e) * get(D2, f)

    def loop(self, number, lo, hi):
        def body(w, carry):
            self.sweep(number, w)
            return carry

        lax.fori_loop(lo, hi, body, 0)


def before_far(own, near, src, st):
    s = Sweeper(st, src)
    s.fill(own, lambda j: 7 - j)
    s.fill(near, lambda j: 8 + j)

    def own_row(w, carry):
        s.coefficients(w, own, lambda l: STORE + l * ROWS + 7 - w, FIXED + 7 - w)
        return carry

    def near_row(w, carry):
        s.coefficients(w, near, lambda l: STORE + l * 3 + w - 8, SENT_FIXED + w - 8)
        return carry

    lax.fori_loop(5, 8, own_row, 0)
    lax.fori_loop(8, 11, near_row, 0)
    s.loop(1, 5, 11)
    s.loop(2, 6, 10)
    s.loop(3, 7, 9)


def after_far(own, far, src, st_in, head_out, sens_out, st):
    del st_in
    me = lax.axis_index("space")
    inside = (me > 0) & (me < lax.axis_size("space") - 1)
    keep = jnp.where(inside, 1.0, 0.0).astype(jnp.float32)
    s = Sweeper(st, src)
    s.fill(far, lambda j: j, keep)

    def far_row(w, carry):
        s.coefficients(
            w, far, lambda l: STORE + l * 3 + w - 1, SENT_FIXED + w - 1, 1.0 - keep
        )
        return carry

    lax.fori_loop(1, 4, far_row, 0)
    s.coefficients(4, own, lambda l: STORE + l * ROWS + 3, FIXED + 3)
    s.loop(1, 1, 5)
    s.loop(2, 2, 6)
    s.loop(3, 3, 7)
    p = odd()

    def last(w, carry):
        r = jnp.where(p == 1, 7 - w, w - 4)
        s.sweep(4, w, (head_out, sens_out, pl.ds(r, SUB, stride=ROWS)))
        return carry

    lax.fori_loop(4, 8, last, 0)


def tiles(x):
    lead, rows, width = x.shape
    x = x.reshape(lead, rows, width // LANE, LANE).transpose(0, 2, 1, 3)
    return x.reshape(lead, rows * width // LANE, LANE)


def rows_back(x, lead):
    x = x.reshape(*lead, SUB, ROWS, LANE)
    x = jnp.swapaxes(x, -3, -2)
    return x.reshape(*lead, ROWS, SUB * LANE)


def local(logk, storage, head0, support, kweight, fixed, directions, wells, rates):
    f32 = jnp.float32
    vmem = pl.BlockSpec(memory_space=pltpu.VMEM)
    hbm = pl.BlockSpec(memory_space=pltpu.HBM)
    logk, storage, head0, support, kweight = map(
        tiles, (logk, storage, head0, support, kweight)
    )
    fixed = tiles(fixed[None])[0]
    table = tiles(directions[None])[0]
    inputs = [
        pltpu.with_memory_space_constraint(x, pltpu.HBM)
        for x in (logk, head0, storage, fixed, support, kweight, table)
    ]
    count = lax.axis_size("space")
    own, near, far = pl.pallas_call(
        gather_pack,
        out_shape=(
            pltpu.VMEM((FULL * SUB, LANE), f32),
            pltpu.VMEM((NEAR * SUB, LANE), f32),
            pltpu.VMEM((FAR * SUB, LANE), f32),
        ),
        in_specs=[hbm] * 7,
        out_specs=(vmem,) * 3,
        scratch_shapes=[pltpu.VMEM(x.shape, x.dtype) for x in inputs]
        + [pltpu.SemaphoreType.DMA((7,))],
        compiler_params=pltpu.CompilerParams(vmem_limit_bytes=VMEM_BYTES),
        name="gather_pack",
    )(*inputs)
    far = lax.ppermute(
        far,
        "space",
        [(i, i + 1 if i % 2 else i - 1) for i in range(1, count - 1)],
    )
    near = lax.ppermute(near, "space", [(i, i ^ 1) for i in range(count)])
    src = pl.pallas_call(
        well_source,
        out_shape=pltpu.VMEM((LAYERS * 10 * SUB, LANE), f32),
        in_specs=[hbm] * 2,
        out_specs=vmem,
        scratch_shapes=[
            pltpu.VMEM((1, wells.shape[0]), wells.dtype),
            pltpu.VMEM((1, rates.shape[0]), rates.dtype),
            pltpu.SemaphoreType.DMA((2,)),
        ],
        compiler_params=pltpu.CompilerParams(vmem_limit_bytes=VMEM_BYTES),
        name="well_source",
    )(*(pltpu.with_memory_space_constraint(x[None], pltpu.HBM) for x in (wells, rates)))
    state = pl.pallas_call(
        before_far,
        out_shape=pltpu.VMEM((STATE * SUB, LANE), f32),
        in_specs=[vmem] * 3,
        out_specs=vmem,
        compiler_params=pltpu.CompilerParams(vmem_limit_bytes=VMEM_BYTES),
        cost_estimate=pl.CostEstimate(flops=0, bytes_accessed=0, transcendentals=0),
        name="before_far",
    )(own, near, src)
    head, sens, _ = pl.pallas_call(
        after_far,
        out_shape=(
            jax.ShapeDtypeStruct((LAYERS, SUB * ROWS, LANE), f32),
            jax.ShapeDtypeStruct((DIRS, LAYERS, SUB * ROWS, LANE), f32),
            pltpu.VMEM((STATE * SUB, LANE), f32),
        ),
        in_specs=[vmem] * 4,
        out_specs=(vmem,) * 3,
        input_output_aliases={3: 2},
        compiler_params=pltpu.CompilerParams(vmem_limit_bytes=VMEM_BYTES),
        name="after_far",
    )(own, far, src, state)
    return rows_back(head, (LAYERS,)), rows_back(sens, (DIRS, LAYERS))


def solution(mesh):
    rows = P(None, "space", None)
    return jax.shard_map(
        local,
        mesh=mesh,
        in_specs=(rows,) * 5 + (P("space", None), P("dir", None), P(), P()),
        out_specs=(rows, P("dir", None, "space", None)),
        check_vma=False,
    )
```

time: 29.5 us -> 22.2 us (0.75)
  the two profiles are of different devices: /device:TPU:255 before, /device:TPU:1 now
where the time goes in v2:
time: 22.2 us; the launch traced here: 22 us
  Pallas kernels  11.8 us (53%)
  starting transfers between devices  9.46 us (43%)
  between operations  0.69 us (3%)
    ppermute x1, starting transfers between devices, local(): lax.ppermute(far, 'space', [(i, i + 1 if i % 2 else i - 1) for i in range...  6.21 us
    pallas_call x1, Pallas kernels, local(): pl.pallas_call(gather_pack, out_shape=(pltpu.VMEM((FULL * SUB, LANE), f32...  4.63 us
    ppermute x1, starting transfers between devices, local(): near = lax.ppermute(near, 'space', [(i, i ^ 1) for i in range(count)])  3.25 us
    pallas_call x1, Pallas kernels, local(): pl.pallas_call(after_far, out_shape=(jax.ShapeDtypeStruct((LAYERS, SUB *...  3.03 us
    pallas_call x1, Pallas kernels, local(): pl.pallas_call(well_source, out_shape=pltpu.VMEM((LAYERS * 10 * SUB, LANE...  2.1 us
    pallas_call x1, Pallas kernels, local(): pl.pallas_call(before_far, out_shape=pltpu.VMEM((STATE * SUB, LANE), f32)...  2.05 us
  transfers between devices with their start and end apart: 2, of which 0 were waited for; matrix products, arithmetic and copies ran while one was open for 0% of the time, Pallas kernels for 19%

profile of v2, /device:TPU:1, one launch (start us, length us, event | category | flops | bytes accessed | tf_op | source)
XLA Modules:
  0.0 22.0 jit_solution(10654925402781995504)
XLA Ops:
  0.6 4.6 %gather_pack.1 = (f32[544,128]{1,0:T(8,128)S(1)}, f32[504,128]{1,0:T(8,128)S(1)}, f32[512,128]{1,0:T(8,128)S(1)}) custom-call(f32[4,32,128]{2,1,0:T(8,128)} %bitcast.47, f32[4,32,128]{2,1,0:T(8,128)} %bitcast.48, f32[4,32,128]{2,1,0:T(8,128)} %bitcast.49, s32[32,128]{1,0:T(8,128)} %bitcast.53, s32[4,32,128]{2,1,0:T(8,128)} %bitcast.50, ...), custom_call_target="tpu_custom_call" | custom-call | tf_op jit(solution)/shard_map/gather_pack/pallas_call | solution.py:364
  5.3 6.2 %collective-permute-start = (f32[512,128]{1,0:T(8,128)S(1)}, f32[512,128]{1,0:T(8,128)S(1)}, u32[]{:S(2)}, u32[]{:S(2)}) collective-permute-start(f32[512,128]{1,0:T(8,128)S(1)} %get-tuple-element.8), channel_id=1, source_target_pairs={{1,2},{2,1},{3,4},{4,3},{5,6},{6,5},{7,8},{8,7},{9,10},{10,9},{11,... | collective-permute-start | bytes 786440 | tf_op jit(solution)/shard_map/ppermute | solution.py:378
  11.5 3.3 %collective-permute-start.1 = (f32[504,128]{1,0:T(8,128)S(1)}, f32[504,128]{1,0:T(8,128)S(1)}, u32[]{:S(2)}, u32[]{:S(2)}) collective-permute-start(f32[504,128]{1,0:T(8,128)S(1)} %get-tuple-element.9), channel_id=1, source_target_pairs={{0,1},{1,0},{2,3},{3,2},{4,5},{5,4},{6,7},{7,6},{8,9},{9,8},{10,11... | collective-permute-start | bytes 774152 | tf_op jit(solution)/shard_map/ppermute | solution.py:383
  14.7 2.1 %well_source.1.src = f32[320,128]{1,0:T(8,128)S(1)} custom-call(s32[1,1024]{1,0:T(1,128)} %bitcast.54, f32[1,1024]{1,0:T(1,128)} %bitcast.55), custom_call_target="tpu_custom_call" | custom-call | tf_op jit(solution)/shard_map/well_source/pallas_call | solution.py:384
  16.9 0.0 collective-permute-done.1.near
  16.9 2.1 %before_far.1.st_in = f32[11520,128]{1,0:T(8,128)S(1)} custom-call(f32[544,128]{1,0:T(8,128)S(1)} %get-tuple-element.7.own, f32[504,128]{1,0:T(8,128)S(1)} %collective-permute-done.1.near, f32[320,128]{1,0:T(8,128)S(1)} %well_source.1.src), custom_call_target="tpu_custom_call" | custom-call | tf_op jit(solution)/shard_map/before_far/pallas_call | solution.py:397
  18.9 0.0 collective-permute-done.far
  18.9 3.0 %after_far.1 = (f32[4,32,128]{2,1,0:T(8,128)}, f32[4,4,32,128]{3,2,1,0:T(8,128)}, f32[11520,128]{1,0:T(8,128)S(1)}) custom-call(f32[544,128]{1,0:T(8,128)S(1)} %get-tuple-element.7.own, f32[512,128]{1,0:T(8,128)S(1)} %collective-permute-done.far, f32[320,128]{1,0:T(8,128)S(1)} %well_source.1.src, ...), custom_call_target="tpu_custom_call", output_to_operand_aliasing={{2}: (3, {})} | custom-call | tf_op jit(solution)/shard_map/after_far/pallas_call | solution.py:406
Async XLA Ops:
  5.3 13.7 %collective-permute-start = (f32[512,128]{1,0:T(8,128)S(1)}, f32[512,128]{1,0:T(8,128)S(1)}, u32[]{:S(2)}, u32[]{:S(2)}) collective-permute-start(f32[512,128]{1,0:T(8,128)S(1)} %get-tuple-element.8), channel_id=1, source_target_pairs={{1,2},{2,1},{3,4},{4,3},{5,6},{6,5},{7,8},{8,7},{9,10},{10,9},{11,... | collective-permute-start | bytes 786440 | tf_op jit(solution)/shard_map/ppermute | solution.py:378
  11.5 5.4 %collective-permute-start.1 = (f32[504,128]{1,0:T(8,128)S(1)}, f32[504,128]{1,0:T(8,128)S(1)}, u32[]{:S(2)}, u32[]{:S(2)}) collective-permute-start(f32[504,128]{1,0:T(8,128)S(1)} %get-tuple-element.9), channel_id=1, source_target_pairs={{0,1},{1,0},{2,3},{3,2},{4,5},{5,4},{6,7},{7,6},{8,9},{9,8},{10,11... | collective-permute-start | bytes 774152 | tf_op jit(solution)/shard_map/ppermute | solution.py:383

commit v3 on v2

--- a/solution.py
+++ b/solution.py
@@ -49,7 +49,7 @@
     t = dirs[...]
     t_high = t.astype(jnp.bfloat16)
     t_low = (t - t_high.astype(jnp.float32)).astype(jnp.bfloat16)
-    left = jnp.concatenate([t_high, t_low], axis=1)
+    left = jnp.concatenate([t_high, t_low], axis=0)
     banks = dirs.shape[0] // DIRS
     places = lax.broadcasted_iota(jnp.int32, (LANE, LANE), 0).astype(jnp.bfloat16)
     half = lax.broadcasted_iota(jnp.int32, (SUB, LANE), 0) >> 2
@@ -71,8 +71,8 @@
                 high.append((idx >> 7) - half)
                 weight.append(jnp.broadcast_to(kwei[s, pl.ds(at, 1), :], (SUB, LANE)))
             right = jnp.concatenate(hot, axis=1)
-            right = jnp.concatenate([right, right], axis=0)
             found = jnp.dot(left, right, preferred_element_type=jnp.float32)
+            found = found[: banks * DIRS] + found[banks * DIRS :]
             for h in range(2):
                 value = jnp.zeros((SUB, LANE), jnp.float32)
                 for m in range(banks // 2):
@@ -88,7 +88,7 @@
             far[pl.ds(at, DIRS, stride=ROWS * SUB), :] = done
         return carry
 
-    lax.fori_loop(0, 4 * ROWS, block, 0)
+    lax.fori_loop(0, 4 * ROWS, block, 0, unroll=True)
     for load in loads[:4]:
         load.wait()
     far[tile(NEAR), :] = jnp.zeros((SUB, LANE), jnp.float32)
@@ -137,15 +137,21 @@
     count = w.shape[1]
     rows = out.shape[0]
     hit = lax.broadcasted_iota(jnp.int32, (rows, count), 0) == place
-    left = jnp.where(hit, jnp.broadcast_to(rates[...], (rows, count)), 0.0)
+    left = hit.astype(jnp.float32).astype(jnp.bfloat16)
     lane = lax.broadcasted_iota(jnp.int32, (LANE, count), 0) == (w & (LANE - 1))
-    out[...] = lax.dot_general(
+    rest = rates[...]
+    parts = []
+    for _ in range(3):
+        part = rest.astype(jnp.bfloat16).astype(jnp.float32)
+        rest = rest - part
+        parts.append(jnp.where(lane, part, 0.0).astype(jnp.bfloat16))
+    total = lax.dot_general(
         left,
-        lane.astype(jnp.float32),
+        jnp.concatenate(parts, axis=0),
         (((1,), (1,)), ((), ())),
-        precision=lax.Precision.HIGHEST,
         preferred_element_type=jnp.float32,
     )
+    out[...] = (total[:, :LANE] + total[:, LANE : 2 * LANE]) + total[:, 2 * LANE :]
 
 
 class Sweeper:
@@ -278,12 +284,9 @@
                 else:
                     outs[1][d, l, outs[2], :] = out + (sc / e) * get(D2, f)
 
-    def loop(self, number, lo, hi):
-        def body(w, carry):
+    def rows(self, number, lo, hi):
+        for w in range(lo, hi):
             self.sweep(number, w)
-            return carry
-
-        lax.fori_loop(lo, hi, body, 0)
 
 
 def before_far(own, near, src, st):
@@ -291,19 +294,13 @@
     s.fill(own, lambda j: 7 - j)
     s.fill(near, lambda j: 8 + j)
 
-    def own_row(w, carry):
+    for w in range(5, 8):
         s.coefficients(w, own, lambda l: STORE + l * ROWS + 7 - w, FIXED + 7 - w)
-        return carry
-
-    def near_row(w, carry):
+    for w in range(8, 11):
         s.coefficients(w, near, lambda l: STORE + l * 3 + w - 8, SENT_FIXED + w - 8)
-        return carry
-
-    lax.fori_loop(5, 8, own_row, 0)
-    lax.fori_loop(8, 11, near_row, 0)
-    s.loop(1, 5, 11)
-    s.loop(2, 6, 10)
-    s.loop(3, 7, 9)
+    s.rows(1, 5, 11)
+    s.rows(2, 6, 10)
+    s.rows(3, 7, 9)
 
 
 def after_far(own, far, src, st_in, head_out, sens_out, st):
@@ -314,25 +311,18 @@
     s = Sweeper(st, src)
     s.fill(far, lambda j: j, keep)
 
-    def far_row(w, carry):
+    for w in range(1, 4):
         s.coefficients(
             w, far, lambda l: STORE + l * 3 + w - 1, SENT_FIXED + w - 1, 1.0 - keep
         )
-        return carry
-
-    lax.fori_loop(1, 4, far_row, 0)
     s.coefficients(4, own, lambda l: STORE + l * ROWS + 3, FIXED + 3)
-    s.loop(1, 1, 5)
-    s.loop(2, 2, 6)
-    s.loop(3, 3, 7)
+    s.rows(1, 1, 5)
+    s.rows(2, 2, 6)
+    s.rows(3, 3, 7)
     p = odd()
-
-    def last(w, carry):
+    for w in range(4, 8):
         r = jnp.where(p == 1, 7 - w, w - 4)
         s.sweep(4, w, (head_out, sens_out, pl.ds(r, SUB, stride=ROWS)))
-        return carry
-
-    lax.fori_loop(4, 8, last, 0)
 
 
 def tiles(x):

time: 22.2 us -> 17.3 us (0.78)
  Pallas kernels: 11.8 us -> 6.3 us
  waiting for transfers between devices: 0.01 us -> 0.65 us
    pallas_call x1, Pallas kernels: 4.63 us -> 2.26 us  [local(): pl.pallas_call(gather_pack, out_shape=(pltpu.VMEM((FULL * SUB, LANE), f32...]
    pallas_call x1, Pallas kernels: 3.03 us -> 1.86 us  [local(): pl.pallas_call(after_far, out_shape=(jax.ShapeDtypeStruct((LAYERS, SUB *...]
    pallas_call x1, Pallas kernels: 2.05 us -> 0.91 us  [local(): pl.pallas_call(before_far, out_shape=pltpu.VMEM((STATE * SUB, LANE), f32)...]
    pallas_call x1, Pallas kernels: 2.1 us -> 1.27 us  [local(): pl.pallas_call(well_source, out_shape=pltpu.VMEM((LAYERS * 10 * SUB, LANE...]
    ppermute x1, waiting for transfers between devices: 0.01 us -> 0.64 us  [local(): lax.ppermute(far, 'space', [(i, i + 1 if i % 2 else i - 1) for i in range...]
  transfers between devices with their start and end apart: 2 -> 2, of which waited for: 0 -> 1; matrix products, arithmetic and copies ran while one was open for 0% -> 0% of each run, Pallas kernels for 19% -> 13%
where the time goes in v3:
time: 17.3 us; the launch traced here: 17.1 us
  starting transfers between devices  9.46 us (55%)
  Pallas kernels  6.3 us (36%)
  between operations  0.68 us (4%)
  waiting for transfers between devices  0.65 us (4%)
    ppermute x1, starting transfers between devices, local(): lax.ppermute(far, 'space', [(i, i + 1 if i % 2 else i - 1) for i in range...  6.21 us
    ppermute x1, starting transfers between devices, local(): near = lax.ppermute(near, 'space', [(i, i ^ 1) for i in range(count)])  3.25 us
    pallas_call x1, Pallas kernels, local(): pl.pallas_call(gather_pack, out_shape=(pltpu.VMEM((FULL * SUB, LANE), f32...  2.26 us
    pallas_call x1, Pallas kernels, local(): pl.pallas_call(after_far, out_shape=(jax.ShapeDtypeStruct((LAYERS, SUB *...  1.86 us
    pallas_call x1, Pallas kernels, local(): pl.pallas_call(well_source, out_shape=pltpu.VMEM((LAYERS * 10 * SUB, LANE...  1.27 us
    pallas_call x1, Pallas kernels, local(): pl.pallas_call(before_far, out_shape=pltpu.VMEM((STATE * SUB, LANE), f32)...  0.91 us
    ppermute x1, waiting for transfers between devices, local(): lax.ppermute(far, 'space', [(i, i + 1 if i % 2 else i - 1) for i in range...  0.64 us
  transfers between devices with their start and end apart: 2, of which 1 were waited for; matrix products, arithmetic and copies ran while one was open for 0% of the time, Pallas kernels for 13%

profile of v3, /device:TPU:1, one launch (start us, length us, event | category | flops | bytes accessed | tf_op | source)
XLA Modules:
  0.0 17.1 jit_solution(5419805117007955371)
XLA Ops:
  0.6 2.3 %gather_pack.1 = (f32[544,128]{1,0:T(8,128)S(1)}, f32[504,128]{1,0:T(8,128)S(1)}, f32[512,128]{1,0:T(8,128)S(1)}) custom-call(f32[4,32,128]{2,1,0:T(8,128)} %bitcast.47, f32[4,32,128]{2,1,0:T(8,128)} %bitcast.48, f32[4,32,128]{2,1,0:T(8,128)} %bitcast.49, s32[32,128]{1,0:T(8,128)} %bitcast.53, s32[4,32,128]{2,1,0:T(8,128)} %bitcast.50, ...), custom_call_target="tpu_custom_call" | custom-call | tf_op jit(solution)/shard_map/gather_pack/pallas_call | solution.py:354
  2.9 6.2 %collective-permute-start = (f32[512,128]{1,0:T(8,128)S(1)}, f32[512,128]{1,0:T(8,128)S(1)}, u32[]{:S(2)}, u32[]{:S(2)}) collective-permute-start(f32[512,128]{1,0:T(8,128)S(1)} %get-tuple-element.8), channel_id=1, source_target_pairs={{1,2},{2,1},{3,4},{4,3},{5,6},{6,5},{7,8},{8,7},{9,10},{10,9},{11,... | collective-permute-start | bytes 786440 | tf_op jit(solution)/shard_map/ppermute | solution.py:368
  9.1 3.3 %collective-permute-start.1 = (f32[504,128]{1,0:T(8,128)S(1)}, f32[504,128]{1,0:T(8,128)S(1)}, u32[]{:S(2)}, u32[]{:S(2)}) collective-permute-start(f32[504,128]{1,0:T(8,128)S(1)} %get-tuple-element.9), channel_id=1, source_target_pairs={{0,1},{1,0},{2,3},{3,2},{4,5},{5,4},{6,7},{7,6},{8,9},{9,8},{10,11... | collective-permute-start | bytes 774152 | tf_op jit(solution)/shard_map/ppermute | solution.py:373
  12.4 1.3 %well_source.1.src = f32[320,128]{1,0:T(8,128)S(1)} custom-call(s32[1,1024]{1,0:T(1,128)} %bitcast.54, f32[1,1024]{1,0:T(1,128)} %bitcast.55), custom_call_target="tpu_custom_call" | custom-call | tf_op jit(solution)/shard_map/well_source/pallas_call | solution.py:374
  13.7 0.0 collective-permute-done.1.near
  13.7 0.9 %before_far.1.st_in = f32[11520,128]{1,0:T(8,128)S(1)} custom-call(f32[544,128]{1,0:T(8,128)S(1)} %get-tuple-element.7.own, f32[504,128]{1,0:T(8,128)S(1)} %collective-permute-done.1.near, f32[320,128]{1,0:T(8,128)S(1)} %well_source.1.src), custom_call_target="tpu_custom_call" | custom-call | tf_op jit(solution)/shard_map/before_far/pallas_call | solution.py:387
  14.6 0.6 %collective-permute-done.far = f32[512,128]{1,0:T(8,128)S(1)} collective-permute-done((f32[512,128]{1,0:T(8,128)S(1)}, f32[512,128]{1,0:T(8,128)S(1)}, u32[]{:S(2)}, u32[]{:S(2)}) %collective-permute-start) | collective-permute-done | bytes 262176 | tf_op jit(solution)/shard_map/ppermute | solution.py:368
  15.2 1.9 %after_far.1 = (f32[4,32,128]{2,1,0:T(8,128)}, f32[4,4,32,128]{3,2,1,0:T(8,128)}, f32[11520,128]{1,0:T(8,128)S(1)}) custom-call(f32[544,128]{1,0:T(8,128)S(1)} %get-tuple-element.7.own, f32[512,128]{1,0:T(8,128)S(1)} %collective-permute-done.far, f32[320,128]{1,0:T(8,128)S(1)} %well_source.1.src, ...), custom_call_target="tpu_custom_call", output_to_operand_aliasing={{2}: (3, {})} | custom-call | tf_op jit(solution)/shard_map/after_far/pallas_call | solution.py:396
Async XLA Ops:
  2.9 12.3 %collective-permute-start = (f32[512,128]{1,0:T(8,128)S(1)}, f32[512,128]{1,0:T(8,128)S(1)}, u32[]{:S(2)}, u32[]{:S(2)}) collective-permute-start(f32[512,128]{1,0:T(8,128)S(1)} %get-tuple-element.8), channel_id=1, source_target_pairs={{1,2},{2,1},{3,4},{4,3},{5,6},{6,5},{7,8},{8,7},{9,10},{10,9},{11,... | collective-permute-start | bytes 786440 | tf_op jit(solution)/shard_map/ppermute | solution.py:368
  9.1 4.5 %collective-permute-start.1 = (f32[504,128]{1,0:T(8,128)S(1)}, f32[504,128]{1,0:T(8,128)S(1)}, u32[]{:S(2)}, u32[]{:S(2)}) collective-permute-start(f32[504,128]{1,0:T(8,128)S(1)} %get-tuple-element.9), channel_id=1, source_target_pairs={{0,1},{1,0},{2,3},{3,2},{4,5},{5,4},{6,7},{7,6},{8,9},{9,8},{10,11... | collective-permute-start | bytes 774152 | tf_op jit(solution)/shard_map/ppermute | solution.py:373

commit v4 on v3

--- a/solution.py
+++ b/solution.py
@@ -9,6 +9,7 @@
 LAYERS, ROWS, DIRS, SUPPORT = 4, 4, 4, 4
 WIDE = 3 * ROWS
 VERTICAL = 0.3
+BY_LANES = 1
 VMEM_BYTES = 16 * 2**20
 
 LOGK, HEAD, DLK, STORE, FIXED, FULL = 0, 16, 32, 48, 64, 68
@@ -20,7 +21,9 @@
 DLU, DLD = DL + PLANE, DL + 2 * PLANE
 KK = DL + 3 * PLANE
 D1, D2, D3 = KK + FIELD, KK + 2 * FIELD, KK + 3 * FIELD
-STATE = KK + 4 * FIELD
+HALF = LAYERS + DIRS * LAYERS
+EARLY = KK + 4 * FIELD
+STATE = EARLY + 4 * HALF
 
 
 def tile(k):
@@ -88,7 +91,33 @@
             far[pl.ds(at, DIRS, stride=ROWS * SUB), :] = done
         return carry
 
-    lax.fori_loop(0, 4 * ROWS, block, 0, unroll=True)
+    def by_lanes(j):
+        r = source_row(j)
+        rows = pl.ds(r, SUB, stride=ROWS)
+        idx = [supp[s, rows, :] for s in range(SUPPORT)]
+        low = [i & (LANE - 1) for i in idx]
+        high = [i >> 7 for i in idx]
+        found = [[jnp.zeros((SUB, LANE), jnp.float32)] * DIRS for _ in idx]
+        for k in range(banks):
+            hit = [h == k for h in high]
+            for d in range(DIRS):
+                bank = jnp.broadcast_to(dirs[pl.ds(k * DIRS + d, 1), :], (SUB, LANE))
+                for s in range(SUPPORT):
+                    g = jnp.take_along_axis(bank, low[s], axis=1, mode="promise_in_bounds")
+                    found[s][d] = jnp.where(hit[s], g, found[s][d])
+        weight = [kwei[s, rows, :] for s in range(SUPPORT)]
+        for d in range(DIRS):
+            total = found[0][d] * weight[0]
+            for s in range(1, SUPPORT):
+                total = total + found[s][d] * weight[s]
+            for out in (own, near, far):
+                out[tile(DLK + d * ROWS + j), :] = total
+
+    for i in range(4 * ROWS):
+        if i == 0:
+            by_lanes(0)
+        if i >= 4 * BY_LANES:
+            block(i, 0)
     for load in loads[:4]:
         load.wait()
     far[tile(NEAR), :] = jnp.zeros((SUB, LANE), jnp.float32)
@@ -227,62 +256,100 @@
                 k = xp * dl[d][2] + xm * dl[d][0] + yp * dlu[d] + ym * dld[d] + tall * dl[d][1]
                 self.put(KK, (d * LAYERS + l) * WIDE + w, k)
 
-    def sweep(self, number, w, outs=None):
+    def base_sides(self, number, w):
+        prev = (G0, G1, G2, G3)[number - 1]
+        here = [self.get(prev, l * WIDE + w) for l in range(LAYERS)]
+        return [
+            (self.get(prev, l * WIDE + w + 1), self.up(g), self.down(g), self.tall(here, l))
+            for l, g in enumerate(here)
+        ]
+
+    def tall(self, here, l):
+        beside = [here[k] for k in (l - 1, l + 1) if 0 <= k < LAYERS]
+        return VERTICAL * (beside[0] if len(beside) == 1 else beside[0] + beside[1])
+
+    def tangent_sides(self, number, w, d, sides):
+        dprev = (None, D1, D2, D3)[number - 1]
+        p = d * WIDE + w
+        here, after = self.get(DL, p), self.get(DL, p + 1)
+        plus, minus = self.get(DLU, p), self.get(DLD, p)
+        sums = [(xp * after + tall * here) + (yp * plus + ym * minus) for xp, yp, ym, tall in sides]
+        if dprev is not None:
+            at = [(d * LAYERS + l) * WIDE + w for l in range(LAYERS)]
+            v = [self.get(dprev, f) for f in at]
+            sums = [
+                acc + ((self.up(v[l]) + self.down(v[l])) + (self.get(dprev, at[l] + 1) + self.tall(v, l)))
+                for l, acc in enumerate(sums)
+            ]
+        return sums
+
+    def early(self, number, w):
+        at = (number - 1) * HALF
+        sides = self.base_sides(number, w)
+        for l, (xp, yp, ym, tall) in enumerate(sides):
+            self.put(EARLY, at + l, (xp + tall) + (yp + ym))
+        for d in range(DIRS):
+            for l, acc in enumerate(self.tangent_sides(number, w, d, sides)):
+                self.put(EARLY, at + LAYERS + d * LAYERS + l, acc)
+
+    def base_row(self, number, w, late=False, out=None):
         start = H0 if number < 3 else H2
         prev = (G0, G1, G2, G3)[number - 1]
         new = (G1, G2, G3, None)[number - 1]
-        dprev = (None, D1, D2, D3)[number - 1]
-        dnew = (D1, D2, D3, None)[number - 1]
         get = self.get
-        dl = [[get(DL, d * WIDE + w + o) for o in (-1, 0, 1)] for d in range(DIRS)]
-        dlu = [get(DLU, d * WIDE + w) for d in range(DIRS)]
-        dld = [get(DLD, d * WIDE + w) for d in range(DIRS)]
+        at = (number - 1) * HALF
+        sides = None if late else self.base_sides(number, w)
+        base = []
         for l in range(LAYERS):
             i = l * WIDE + w
-            here = get(prev, i)
-            xp, xm = get(prev, i + 1), get(prev, i - 1)
-            yp, ym = self.up(here), self.down(here)
-            tall = None
-            if l < LAYERS - 1:
-                tall = get(prev, i + WIDE)
-            if l > 0:
-                below = get(prev, i - WIDE)
-                tall = below if tall is None else tall + below
-            tall = VERTICAL * tall
-            total = ((xp + xm) + (yp + ym)) + tall
+            if late:
+                total = get(EARLY, at + l)
+            else:
+                xp, yp, ym, tall = sides[l]
+                total = (xp + tall) + (yp + ym)
+            xm = get(prev, i - 1)
+            total = total + xm
             e, sc, pp = get(E, i), get(SC, i), get(PP, i)
             value = sc * get(start, i) + get(SW, i) + pp * total
             if new is not None:
                 self.put(new, i, e * value)
             if number == 2:
                 self.put(H2, i, value)
-            if outs is not None:
-                outs[0][l, outs[2], :] = value
-            own = (total - value * get(S0, i)) + tall
-            scaled = pp if outs is not None else pp * e
-            for d in range(DIRS):
-                f = (d * LAYERS + l) * WIDE + w
-                acc = own * dl[d][1] - value * get(KK, f)
-                acc = acc + (xp * dl[d][2] + xm * dl[d][0])
-                acc = acc + (yp * dlu[d] + ym * dld[d])
-                if dprev is not None:
-                    v = get(dprev, f)
-                    acc = acc + (get(dprev, f + 1) + get(dprev, f - 1))
-                    acc = acc + (self.up(v) + self.down(v))
-                    side = None
-                    if l < LAYERS - 1:
-                        side = get(dprev, f + WIDE)
-                    if l > 0:
-                        below = get(dprev, f - WIDE)
-                        side = below if side is None else side + below
-                    acc = acc + VERTICAL * side
-                out = scaled * acc
-                if number == 3:
-                    out = out + sc * get(D2, f)
-                if dnew is not None:
-                    self.put(dnew, f, out)
-                else:
-                    outs[1][d, l, outs[2], :] = out + (sc / e) * get(D2, f)
+            if out is not None:
+                out[0][l, out[1], :] = value
+            scaled, kept = (pp, sc / e) if out is not None else (pp * e, sc)
+            base.append((xm, value, total - value * get(S0, i), scaled, kept))
+        return sides, base
+
+    def tangent_row(self, number, w, d, sides, base, out=None):
+        dprev = (None, D1, D2, D3)[number - 1]
+        dnew = (D1, D2, D3, None)[number - 1]
+        get = self.get
+        if sides is None:
+            at = (number - 1) * HALF + LAYERS + d * LAYERS
+            sums = [get(EARLY, at + l) for l in range(LAYERS)]
+        else:
+            sums = self.tangent_sides(number, w, d, sides)
+        p = d * WIDE + w
+        here, before = get(DL, p), get(DL, p - 1)
+        for l, (xm, value, own, scaled, kept) in enumerate(base):
+            f = (d * LAYERS + l) * WIDE + w
+            acc = sums[l] + xm * before
+            if dprev is not None:
+                acc = acc + get(dprev, f - 1)
+            acc = acc + (own * here - value * get(KK, f))
+            result = scaled * acc
+            if number > 2:
+                result = result + kept * get(D2, f)
+            if out is None:
+                self.put(dnew, f, result)
+            else:
+                out[0][d, l, out[1], :] = result
+
+    def sweep(self, number, w, late=False):
+        sides, base = self.base_row(number, w, late)
+        for d in range(DIRS):
+            self.tangent_row(number, w, d, sides, base)
 
     def rows(self, number, lo, hi):
         for w in range(lo, hi):
@@ -301,9 +368,11 @@
     s.rows(1, 5, 11)
     s.rows(2, 6, 10)
     s.rows(3, 7, 9)
-
-
-def after_far(own, far, src, st_in, head_out, sens_out, st):
+    for number in range(1, 5):
+        s.early(number, number + 3)
+
+
+def after_far(own, far, src, st_in, head_out, sens_out, st, head, sens, sem):
     del st_in
     me = lax.axis_index("space")
     inside = (me > 0) & (me < lax.axis_size("space") - 1)
@@ -316,13 +385,21 @@
             w, far, lambda l: STORE + l * 3 + w - 1, SENT_FIXED + w - 1, 1.0 - keep
         )
     s.coefficients(4, own, lambda l: STORE + l * ROWS + 3, FIXED + 3)
-    s.rows(1, 1, 5)
-    s.rows(2, 2, 6)
-    s.rows(3, 3, 7)
+    for number in range(1, 4):
+        s.rows(number, number, number + 3)
+        s.sweep(number, number + 3, late=True)
     p = odd()
-    for w in range(4, 8):
-        r = jnp.where(p == 1, 7 - w, w - 4)
-        s.sweep(4, w, (head_out, sens_out, pl.ds(r, SUB, stride=ROWS)))
+    rows = {w: pl.ds(jnp.where(p == 1, 7 - w, w - 4), SUB, stride=ROWS) for w in range(4, 8)}
+    base = {w: s.base_row(4, w, w == 7, (head, rows[w])) for w in rows}
+    stores = [pltpu.make_async_copy(head, head_out, sem.at[DIRS])]
+    stores[0].start()
+    for d in range(DIRS):
+        for w in rows:
+            s.tangent_row(4, w, d, *base[w], (sens, rows[w]))
+        stores.append(pltpu.make_async_copy(sens.at[d], sens_out.at[d], sem.at[d]))
+        stores[-1].start()
+    for store in stores:
+        store.wait()
 
 
 def tiles(x):
@@ -396,12 +473,17 @@
     head, sens, _ = pl.pallas_call(
         after_far,
         out_shape=(
-            jax.ShapeDtypeStruct((LAYERS, SUB * ROWS, LANE), f32),
-            jax.ShapeDtypeStruct((DIRS, LAYERS, SUB * ROWS, LANE), f32),
+            pltpu.HBM((LAYERS, SUB * ROWS, LANE), f32),
+            pltpu.HBM((DIRS, LAYERS, SUB * ROWS, LANE), f32),
             pltpu.VMEM((STATE * SUB, LANE), f32),
         ),
         in_specs=[vmem] * 4,
-        out_specs=(vmem,) * 3,
+        out_specs=(hbm, hbm, vmem),
+        scratch_shapes=[
+            pltpu.VMEM((LAYERS, SUB * ROWS, LANE), f32),
+            pltpu.VMEM((DIRS, LAYERS, SUB * ROWS, LANE), f32),
+            pltpu.SemaphoreType.DMA((DIRS + 1,)),
+        ],
         input_output_aliases={3: 2},
         compiler_params=pltpu.CompilerParams(vmem_limit_bytes=VMEM_BYTES),
         name="after_far",

time: 17.3 us -> 16.9 us (0.977)
  waiting for transfers between devices: 0.65 us -> 0.41 us
    pallas_call x1, Pallas kernels: 2.26 us -> 2 us  [local(): pl.pallas_call(gather_pack, out_shape=(pltpu.VMEM((FULL * SUB, LANE), f32...]
    pallas_call x1, Pallas kernels: 0.91 us -> 1.14 us  [local(): pl.pallas_call(before_far, out_shape=pltpu.VMEM((STATE * SUB, LANE), f32)...]
    ppermute x1, waiting for transfers between devices: 0.64 us -> 0.41 us  [local(): lax.ppermute(far, 'space', [(i, i + 1 if i % 2 else i - 1) for i in range...]
  transfers between devices with their start and end apart: 2 -> 2, of which waited for: 1 -> 1; matrix products, arithmetic and copies ran while one was open for 0% -> 0% of each run, Pallas kernels for 13% -> 14%
where the time goes in v4:
time: 16.9 us; the launch traced here: 16.7 us
  starting transfers between devices  9.46 us (56%)
  Pallas kernels  6.16 us (36%)
  between operations  0.68 us (4%)
  waiting for transfers between devices  0.41 us (2%)
    ppermute x1, starting transfers between devices, local(): lax.ppermute(far, 'space', [(i, i + 1 if i % 2 else i - 1) for i in range...  6.21 us
    ppermute x1, starting transfers between devices, local(): near = lax.ppermute(near, 'space', [(i, i ^ 1) for i in range(count)])  3.25 us
    pallas_call x1, Pallas kernels, local(): pl.pallas_call(gather_pack, out_shape=(pltpu.VMEM((FULL * SUB, LANE), f32...  2 us
    pallas_call x1, Pallas kernels, local(): pl.pallas_call(after_far, out_shape=(pltpu.HBM((LAYERS, SUB * ROWS, LANE)...  1.75 us
    pallas_call x1, Pallas kernels, local(): pl.pallas_call(well_source, out_shape=pltpu.VMEM((LAYERS * 10 * SUB, LANE...  1.27 us
    pallas_call x1, Pallas kernels, local(): pl.pallas_call(before_far, out_shape=pltpu.VMEM((STATE * SUB, LANE), f32)...  1.14 us
    ppermute x1, waiting for transfers between devices, local(): lax.ppermute(far, 'space', [(i, i + 1 if i % 2 else i - 1) for i in range...  0.41 us
  transfers between devices with their start and end apart: 2, of which 1 were waited for; matrix products, arithmetic and copies ran while one was open for 0% of the time, Pallas kernels for 14%

profile of v4, /device:TPU:1, one launch (start us, length us, event | category | flops | bytes accessed | tf_op | source)
XLA Modules:
  0.0 16.7 jit_solution(4542997164992062733)
XLA Ops:
  0.6 2.0 %gather_pack.1 = (f32[544,128]{1,0:T(8,128)S(1)}, f32[504,128]{1,0:T(8,128)S(1)}, f32[512,128]{1,0:T(8,128)S(1)}) custom-call(f32[4,32,128]{2,1,0:T(8,128)} %bitcast.47, f32[4,32,128]{2,1,0:T(8,128)} %bitcast.48, f32[4,32,128]{2,1,0:T(8,128)} %bitcast.49, s32[32,128]{1,0:T(8,128)} %bitcast.53, s32[4,32,128]{2,1,0:T(8,128)} %bitcast.50, ...), custom_call_target="tpu_custom_call" | custom-call | tf_op jit(solution)/shard_map/gather_pack/pallas_call | solution.py:431
  2.6 6.2 %collective-permute-start = (f32[512,128]{1,0:T(8,128)S(1)}, f32[512,128]{1,0:T(8,128)S(1)}, u32[]{:S(2)}, u32[]{:S(2)}) collective-permute-start(f32[512,128]{1,0:T(8,128)S(1)} %get-tuple-element.8), channel_id=1, source_target_pairs={{1,2},{2,1},{3,4},{4,3},{5,6},{6,5},{7,8},{8,7},{9,10},{10,9},{11,... | collective-permute-start | bytes 786440 | tf_op jit(solution)/shard_map/ppermute | solution.py:445
  8.9 3.3 %collective-permute-start.1 = (f32[504,128]{1,0:T(8,128)S(1)}, f32[504,128]{1,0:T(8,128)S(1)}, u32[]{:S(2)}, u32[]{:S(2)}) collective-permute-start(f32[504,128]{1,0:T(8,128)S(1)} %get-tuple-element.9), channel_id=1, source_target_pairs={{0,1},{1,0},{2,3},{3,2},{4,5},{5,4},{6,7},{7,6},{8,9},{9,8},{10,11... | collective-permute-start | bytes 774152 | tf_op jit(solution)/shard_map/ppermute | solution.py:450
  12.1 1.3 %well_source.1.src = f32[320,128]{1,0:T(8,128)S(1)} custom-call(s32[1,1024]{1,0:T(1,128)} %bitcast.54, f32[1,1024]{1,0:T(1,128)} %bitcast.55), custom_call_target="tpu_custom_call" | custom-call | tf_op jit(solution)/shard_map/well_source/pallas_call | solution.py:451
  13.4 0.0 collective-permute-done.1.near
  13.4 1.1 %before_far.1.st_in = f32[12160,128]{1,0:T(8,128)S(1)} custom-call(f32[544,128]{1,0:T(8,128)S(1)} %get-tuple-element.7.own, f32[504,128]{1,0:T(8,128)S(1)} %collective-permute-done.1.near, f32[320,128]{1,0:T(8,128)S(1)} %well_source.1.src), custom_call_target="tpu_custom_call" | custom-call | tf_op jit(solution)/shard_map/before_far/pallas_call | solution.py:464
  14.6 0.4 %collective-permute-done.far = f32[512,128]{1,0:T(8,128)S(1)} collective-permute-done((f32[512,128]{1,0:T(8,128)S(1)}, f32[512,128]{1,0:T(8,128)S(1)}, u32[]{:S(2)}, u32[]{:S(2)}) %collective-permute-start) | collective-permute-done | bytes 262176 | tf_op jit(solution)/shard_map/ppermute | solution.py:445
  15.0 1.8 %after_far.1 = (f32[4,32,128]{2,1,0:T(8,128)}, f32[4,4,32,128]{3,2,1,0:T(8,128)}, f32[12160,128]{1,0:T(8,128)S(1)}) custom-call(f32[544,128]{1,0:T(8,128)S(1)} %get-tuple-element.7.own, f32[512,128]{1,0:T(8,128)S(1)} %collective-permute-done.far, f32[320,128]{1,0:T(8,128)S(1)} %well_source.1.src, ...), custom_call_target="tpu_custom_call", output_to_operand_aliasing={{2}: (3, {})} | custom-call | tf_op jit(solution)/shard_map/after_far/pallas_call | solution.py:473
Async XLA Ops:
  2.6 12.3 %collective-permute-start = (f32[512,128]{1,0:T(8,128)S(1)}, f32[512,128]{1,0:T(8,128)S(1)}, u32[]{:S(2)}, u32[]{:S(2)}) collective-permute-start(f32[512,128]{1,0:T(8,128)S(1)} %get-tuple-element.8), channel_id=1, source_target_pairs={{1,2},{2,1},{3,4},{4,3},{5,6},{6,5},{7,8},{8,7},{9,10},{10,9},{11,... | collective-permute-start | bytes 786440 | tf_op jit(solution)/shard_map/ppermute | solution.py:445
  8.9 4.5 %collective-permute-start.1 = (f32[504,128]{1,0:T(8,128)S(1)}, f32[504,128]{1,0:T(8,128)S(1)}, u32[]{:S(2)}, u32[]{:S(2)}) collective-permute-start(f32[504,128]{1,0:T(8,128)S(1)} %get-tuple-element.9), channel_id=1, source_target_pairs={{0,1},{1,0},{2,3},{3,2},{4,5},{5,4},{6,7},{7,6},{8,9},{9,8},{10,11... | collective-permute-start | bytes 774152 | tf_op jit(solution)/shard_map/ppermute | solution.py:450

commit v5 on v4

--- a/solution.py
+++ b/solution.py
@@ -9,10 +9,10 @@
 LAYERS, ROWS, DIRS, SUPPORT = 4, 4, 4, 4
 WIDE = 3 * ROWS
 VERTICAL = 0.3
-BY_LANES = 1
+BY_LANES = (4, 1, 0, 0)
 VMEM_BYTES = 16 * 2**20
 
-LOGK, HEAD, DLK, STORE, FIXED, FULL = 0, 16, 32, 48, 64, 68
+ROOT, HEAD, DLK, STORE, FIXED, FULL = 0, 16, 32, 48, 64, 68
 SENT_FIXED, NEAR, FAR = 60, 63, 64
 
 GRID, PLANE, FIELD = LAYERS * WIDE, DIRS * WIDE, DIRS * LAYERS * WIDE
@@ -23,7 +23,8 @@
 D1, D2, D3 = KK + FIELD, KK + 2 * FIELD, KK + 3 * FIELD
 HALF = LAYERS + DIRS * LAYERS
 EARLY = KK + 4 * FIELD
-STATE = EARLY + 4 * HALF
+RR = EARLY + 4 * HALF
+STATE = RR + LAYERS * ROWS
 
 
 def tile(k):
@@ -58,11 +59,10 @@
     half = lax.broadcasted_iota(jnp.int32, (SUB, LANE), 0) >> 2
     one, zero = jnp.bfloat16(1), jnp.bfloat16(0)
 
-    def block(i, carry):
-        j, pair = i >> 2, i & 3
+    def block(j, pair):
         r = source_row(j)
         total = [None, None]
-        for s in range(SUPPORT):
+        for s in range(BY_LANES[j], SUPPORT):
             hot, high, weight = [], [], []
             for h in range(2):
                 at = (2 * pair + h) * ROWS + r
@@ -84,17 +84,16 @@
                 value = value * weight[h]
                 total[h] = value if total[h] is None else total[h] + value
         for h in range(2):
-            done = (total[h] + pltpu.roll(total[h], 4, 0))[:DIRS]
+            done = (0.5 * (total[h] + pltpu.roll(total[h], 4, 0)))[:DIRS]
             at = DLK * SUB + j * SUB + 2 * pair + h
-            own[pl.ds(at, DIRS, stride=ROWS * SUB), :] = done
-            near[pl.ds(at, DIRS, stride=ROWS * SUB), :] = done
-            far[pl.ds(at, DIRS, stride=ROWS * SUB), :] = done
-        return carry
+            for out in (own, near, far) if BY_LANES[j] == 0 else (own,):
+                out[pl.ds(at, DIRS, stride=ROWS * SUB), :] = done
 
     def by_lanes(j):
         r = source_row(j)
         rows = pl.ds(r, SUB, stride=ROWS)
-        idx = [supp[s, rows, :] for s in range(SUPPORT)]
+        count = BY_LANES[j]
+        idx = [supp[s, rows, :] for s in range(count)]
         low = [i & (LANE - 1) for i in idx]
         high = [i >> 7 for i in idx]
         found = [[jnp.zeros((SUB, LANE), jnp.float32)] * DIRS for _ in idx]
@@ -102,49 +101,58 @@
             hit = [h == k for h in high]
             for d in range(DIRS):
                 bank = jnp.broadcast_to(dirs[pl.ds(k * DIRS + d, 1), :], (SUB, LANE))
-                for s in range(SUPPORT):
+                for s in range(count):
                     g = jnp.take_along_axis(bank, low[s], axis=1, mode="promise_in_bounds")
                     found[s][d] = jnp.where(hit[s], g, found[s][d])
-        weight = [kwei[s, rows, :] for s in range(SUPPORT)]
+        weight = [0.5 * kwei[s, rows, :] for s in range(count)]
+        totals = []
         for d in range(DIRS):
             total = found[0][d] * weight[0]
-            for s in range(1, SUPPORT):
+            for s in range(1, count):
                 total = total + found[s][d] * weight[s]
-            for out in (own, near, far):
-                out[tile(DLK + d * ROWS + j), :] = total
-
-    for i in range(4 * ROWS):
-        if i == 0:
-            by_lanes(0)
-        if i >= 4 * BY_LANES:
-            block(i, 0)
+            totals.append(total)
+        return totals
+
+    def pack():
+        far[tile(NEAR), :] = jnp.zeros((SUB, LANE), jnp.float32)
+        for j in range(ROWS):
+            r = source_row(j)
+            rows = pl.ds(r, SUB, stride=ROWS)
+            for l in range(LAYERS):
+                k = jnp.exp(0.5 * logk[l, rows, :])
+                h = head[l, rows, :]
+                for out in (own, near, far):
+                    out[tile(ROOT + l * ROWS + j), :] = k
+                    out[tile(HEAD + l * ROWS + j), :] = h
+                s = stor[l, rows, :]
+                own[tile(STORE + l * ROWS + j), :] = s
+                if j > 0:
+                    far[tile(STORE + l * 3 + j - 1), :] = s
+                if j < 3:
+                    near[tile(STORE + l * 3 + j), :] = s
+            f = fixed[rows, :].astype(jnp.float32)
+            own[tile(FIXED + j), :] = f
+            if j > 0:
+                far[tile(SENT_FIXED + j - 1), :] = f
+            if j < 3:
+                near[tile(SENT_FIXED + j), :] = f
+
+    lanes = {j: by_lanes(j) for j in range(ROWS) if BY_LANES[j]}
+    for j in range(ROWS):
+        if BY_LANES[j] < SUPPORT:
+            for pair in range(4):
+                block(j, pair)
+        if BY_LANES[j]:
+            for d in range(DIRS):
+                at = tile(DLK + d * ROWS + j)
+                value = lanes[j][d]
+                if BY_LANES[j] < SUPPORT:
+                    value = value + own[at, :]
+                for out in (own, near, far):
+                    out[at, :] = value
     for load in loads[:4]:
         load.wait()
-    far[tile(NEAR), :] = jnp.zeros((SUB, LANE), jnp.float32)
-    for j in range(ROWS):
-        r = source_row(j)
-        for l in range(LAYERS):
-            rows = pl.ds(r, SUB, stride=ROWS)
-            k = logk[l, rows, :]
-            own[tile(LOGK + l * ROWS + j), :] = k
-            near[tile(LOGK + l * ROWS + j), :] = k
-            far[tile(LOGK + l * ROWS + j), :] = k
-            h = head[l, rows, :]
-            own[tile(HEAD + l * ROWS + j), :] = h
-            near[tile(HEAD + l * ROWS + j), :] = h
-            far[tile(HEAD + l * ROWS + j), :] = h
-            s = stor[l, rows, :]
-            own[tile(STORE + l * ROWS + j), :] = s
-            if j > 0:
-                far[tile(STORE + l * 3 + j - 1), :] = s
-            if j < 3:
-                near[tile(STORE + l * 3 + j), :] = s
-        f = fixed[pl.ds(r, SUB, stride=ROWS), :].astype(jnp.float32)
-        own[tile(FIXED + j), :] = f
-        if j > 0:
-            far[tile(SENT_FIXED + j - 1), :] = f
-        if j < 3:
-            near[tile(SENT_FIXED + j), :] = f
+    pack()
 
 
 def well_source(wells_hbm, rates_hbm, out, wells, rates, sem):
@@ -205,13 +213,11 @@
         edge = jnp.where(self.sub_first, 0.0, pltpu.roll(v, 1, 0))
         return pltpu.roll(jnp.where(self.lane_last, edge, v), 1, 1)
 
-    def fill(self, pack, place, keep=None):
+    def fill(self, pack, place):
         for l in range(LAYERS):
             for j in range(ROWS):
                 i = l * WIDE + place(j)
-                e = jnp.exp(0.5 * pack[tile(LOGK + l * ROWS + j), :])
-                if keep is not None:
-                    e = e * keep
+                e = pack[tile(ROOT + l * ROWS + j), :]
                 h = pack[tile(HEAD + l * ROWS + j), :]
                 self.put(E, i, e)
                 self.put(G0, i, e * h)
@@ -219,7 +225,7 @@
         for d in range(DIRS):
             for j in range(ROWS):
                 i = d * WIDE + place(j)
-                v = 0.5 * pack[tile(DLK + d * ROWS + j), :]
+                v = pack[tile(DLK + d * ROWS + j), :]
                 self.put(DL, i, v)
                 if 0 < place(j) < WIDE - 1:
                     self.put(DLU, i, self.up(v))
@@ -317,7 +323,9 @@
                 self.put(H2, i, value)
             if out is not None:
                 out[0][l, out[1], :] = value
-            scaled, kept = (pp, sc / e) if out is not None else (pp * e, sc)
+            scaled, kept = pp * e, sc
+            if out is not None:
+                scaled, kept = pp, sc * get(RR, l * ROWS + w - 4)
             base.append((xm, value, total - value * get(S0, i), scaled, kept))
         return sides, base
 
@@ -368,6 +376,9 @@
     s.rows(1, 5, 11)
     s.rows(2, 6, 10)
     s.rows(3, 7, 9)
+    for i in range(LAYERS * ROWS):
+        l, w = divmod(i, ROWS)
+        s.put(RR, i, 1.0 / s.get(E, l * WIDE + w + 4))
     for number in range(1, 5):
         s.early(number, number + 3)
 
@@ -376,25 +387,25 @@
     del st_in
     me = lax.axis_index("space")
     inside = (me > 0) & (me < lax.axis_size("space") - 1)
-    keep = jnp.where(inside, 1.0, 0.0).astype(jnp.float32)
+    missing = jnp.where(inside, 0.0, 1.0).astype(jnp.float32)
     s = Sweeper(st, src)
-    s.fill(far, lambda j: j, keep)
+    s.fill(far, lambda j: j)
 
     for w in range(1, 4):
         s.coefficients(
-            w, far, lambda l: STORE + l * 3 + w - 1, SENT_FIXED + w - 1, 1.0 - keep
+            w, far, lambda l: STORE + l * 3 + w - 1, SENT_FIXED + w - 1, missing
         )
     s.coefficients(4, own, lambda l: STORE + l * ROWS + 3, FIXED + 3)
     for number in range(1, 4):
-        s.rows(number, number, number + 3)
-        s.sweep(number, number + 3, late=True)
+        for w in range(number + 3, number - 1, -1):
+            s.sweep(number, w, late=w == number + 3)
     p = odd()
     rows = {w: pl.ds(jnp.where(p == 1, 7 - w, w - 4), SUB, stride=ROWS) for w in range(4, 8)}
     base = {w: s.base_row(4, w, w == 7, (head, rows[w])) for w in rows}
     stores = [pltpu.make_async_copy(head, head_out, sem.at[DIRS])]
     stores[0].start()
     for d in range(DIRS):
-        for w in rows:
+        for w in (5, 6, 7, 4):
             s.tangent_row(4, w, d, *base[w], (sens, rows[w]))
         stores.append(pltpu.make_async_copy(sens.at[d], sens_out.at[d], sem.at[d]))
         stores[-1].start()

time: 16.9 us -> 16.9 us (level)
  no operation moved by 1% of the time
where the time goes in v5:
time: 16.9 us; the launch traced here: 16.6 us
  starting transfers between devices  9.46 us (56%)
  Pallas kernels  6.07 us (36%)
  between operations  0.68 us (4%)
  waiting for transfers between devices  0.42 us (2%)
    ppermute x1, starting transfers between devices, local(): lax.ppermute(far, 'space', [(i, i + 1 if i % 2 else i - 1) for i in range...  6.21 us
    ppermute x1, starting transfers between devices, local(): near = lax.ppermute(near, 'space', [(i, i ^ 1) for i in range(count)])  3.25 us
    pallas_call x1, Pallas kernels, local(): pl.pallas_call(gather_pack, out_shape=(pltpu.VMEM((FULL * SUB, LANE), f32...  1.94 us
    pallas_call x1, Pallas kernels, local(): pl.pallas_call(after_far, out_shape=(pltpu.HBM((LAYERS, SUB * ROWS, LANE)...  1.74 us
    pallas_call x1, Pallas kernels, local(): pl.pallas_call(well_source, out_shape=pltpu.VMEM((LAYERS * 10 * SUB, LANE...  1.27 us
    pallas_call x1, Pallas kernels, local(): pl.pallas_call(before_far, out_shape=pltpu.VMEM((STATE * SUB, LANE), f32)...  1.13 us
    ppermute x1, waiting for transfers between devices, local(): lax.ppermute(far, 'space', [(i, i + 1 if i % 2 else i - 1) for i in range...  0.42 us
  transfers between devices with their start and end apart: 2, of which 1 were waited for; matrix products, arithmetic and copies ran while one was open for 0% of the time, Pallas kernels for 14%

profile of v5, /device:TPU:1, one launch (start us, length us, event | category | flops | bytes accessed | tf_op | source)
XLA Modules:
  0.0 16.6 jit_solution(13962586106424206050)
XLA Ops:
  0.6 1.9 %gather_pack.1 = (f32[544,128]{1,0:T(8,128)S(1)}, f32[504,128]{1,0:T(8,128)S(1)}, f32[512,128]{1,0:T(8,128)S(1)}) custom-call(f32[4,32,128]{2,1,0:T(8,128)} %bitcast.47, f32[4,32,128]{2,1,0:T(8,128)} %bitcast.48, f32[4,32,128]{2,1,0:T(8,128)} %bitcast.49, s32[32,128]{1,0:T(8,128)} %bitcast.53, s32[4,32,128]{2,1,0:T(8,128)} %bitcast.50, ...), custom_call_target="tpu_custom_call" | custom-call | tf_op jit(solution)/shard_map/gather_pack/pallas_call | solution.py:442
  2.6 6.2 %collective-permute-start = (f32[512,128]{1,0:T(8,128)S(1)}, f32[512,128]{1,0:T(8,128)S(1)}, u32[]{:S(2)}, u32[]{:S(2)}) collective-permute-start(f32[512,128]{1,0:T(8,128)S(1)} %get-tuple-element.8), channel_id=1, source_target_pairs={{1,2},{2,1},{3,4},{4,3},{5,6},{6,5},{7,8},{8,7},{9,10},{10,9},{11,... | collective-permute-start | bytes 786440 | tf_op jit(solution)/shard_map/ppermute | solution.py:456
  8.8 3.3 %collective-permute-start.1 = (f32[504,128]{1,0:T(8,128)S(1)}, f32[504,128]{1,0:T(8,128)S(1)}, u32[]{:S(2)}, u32[]{:S(2)}) collective-permute-start(f32[504,128]{1,0:T(8,128)S(1)} %get-tuple-element.9), channel_id=1, source_target_pairs={{0,1},{1,0},{2,3},{3,2},{4,5},{5,4},{6,7},{7,6},{8,9},{9,8},{10,11... | collective-permute-start | bytes 774152 | tf_op jit(solution)/shard_map/ppermute | solution.py:461
  12.1 1.3 %well_source.1.src = f32[320,128]{1,0:T(8,128)S(1)} custom-call(s32[1,1024]{1,0:T(1,128)} %bitcast.54, f32[1,1024]{1,0:T(1,128)} %bitcast.55), custom_call_target="tpu_custom_call" | custom-call | tf_op jit(solution)/shard_map/well_source/pallas_call | solution.py:462
  13.3 0.0 collective-permute-done.1.near
  13.3 1.1 %before_far.1.st_in = f32[12288,128]{1,0:T(8,128)S(1)} custom-call(f32[544,128]{1,0:T(8,128)S(1)} %get-tuple-element.7.own, f32[504,128]{1,0:T(8,128)S(1)} %collective-permute-done.1.near, f32[320,128]{1,0:T(8,128)S(1)} %well_source.1.src), custom_call_target="tpu_custom_call" | custom-call | tf_op jit(solution)/shard_map/before_far/pallas_call | solution.py:475
  14.5 0.4 %collective-permute-done.far = f32[512,128]{1,0:T(8,128)S(1)} collective-permute-done((f32[512,128]{1,0:T(8,128)S(1)}, f32[512,128]{1,0:T(8,128)S(1)}, u32[]{:S(2)}, u32[]{:S(2)}) %collective-permute-start) | collective-permute-done | bytes 262176 | tf_op jit(solution)/shard_map/ppermute | solution.py:456
  14.9 1.7 %after_far.1 = (f32[4,32,128]{2,1,0:T(8,128)}, f32[4,4,32,128]{3,2,1,0:T(8,128)}, f32[12288,128]{1,0:T(8,128)S(1)}) custom-call(f32[544,128]{1,0:T(8,128)S(1)} %get-tuple-element.7.own, f32[512,128]{1,0:T(8,128)S(1)} %collective-permute-done.far, f32[320,128]{1,0:T(8,128)S(1)} %well_source.1.src, ...), custom_call_target="tpu_custom_call", output_to_operand_aliasing={{2}: (3, {})} | custom-call | tf_op jit(solution)/shard_map/after_far/pallas_call | solution.py:484
Async XLA Ops:
  2.6 12.3 %collective-permute-start = (f32[512,128]{1,0:T(8,128)S(1)}, f32[512,128]{1,0:T(8,128)S(1)}, u32[]{:S(2)}, u32[]{:S(2)}) collective-permute-start(f32[512,128]{1,0:T(8,128)S(1)} %get-tuple-element.8), channel_id=1, source_target_pairs={{1,2},{2,1},{3,4},{4,3},{5,6},{6,5},{7,8},{8,7},{9,10},{10,9},{11,... | collective-permute-start | bytes 786440 | tf_op jit(solution)/shard_map/ppermute | solution.py:456
  8.8 4.5 %collective-permute-start.1 = (f32[504,128]{1,0:T(8,128)S(1)}, f32[504,128]{1,0:T(8,128)S(1)}, u32[]{:S(2)}, u32[]{:S(2)}) collective-permute-start(f32[504,128]{1,0:T(8,128)S(1)} %get-tuple-element.9), channel_id=1, source_target_pairs={{0,1},{1,0},{2,3},{3,2},{4,5},{5,4},{6,7},{7,6},{8,9},{9,8},{10,11... | collective-permute-start | bytes 774152 | tf_op jit(solution)/shard_map/ppermute | solution.py:461

commit v6 on v5

--- a/solution.py
+++ b/solution.py
@@ -38,7 +38,7 @@
 
 
 def gather_pack(*refs):
-    hbm, (own, near, far), vmem, sem = refs[:7], refs[7:10], refs[10:17], refs[17]
+    hbm, (own, far), vmem, sem = refs[:7], refs[7:9], refs[9:16], refs[16]
     loads = [pltpu.make_async_copy(a, b, sem.at[i]) for i, (a, b) in enumerate(zip(hbm, vmem))]
     for load in loads[::-1]:
         load.start()
@@ -86,7 +86,7 @@
         for h in range(2):
             done = (0.5 * (total[h] + pltpu.roll(total[h], 4, 0)))[:DIRS]
             at = DLK * SUB + j * SUB + 2 * pair + h
-            for out in (own, near, far) if BY_LANES[j] == 0 else (own,):
+            for out in (own, far) if BY_LANES[j] == 0 else (own,):
                 out[pl.ds(at, DIRS, stride=ROWS * SUB), :] = done
 
     def by_lanes(j):
@@ -121,21 +121,17 @@
             for l in range(LAYERS):
                 k = jnp.exp(0.5 * logk[l, rows, :])
                 h = head[l, rows, :]
-                for out in (own, near, far):
+                for out in (own, far):
                     out[tile(ROOT + l * ROWS + j), :] = k
                     out[tile(HEAD + l * ROWS + j), :] = h
                 s = stor[l, rows, :]
                 own[tile(STORE + l * ROWS + j), :] = s
                 if j > 0:
                     far[tile(STORE + l * 3 + j - 1), :] = s
-                if j < 3:
-                    near[tile(STORE + l * 3 + j), :] = s
             f = fixed[rows, :].astype(jnp.float32)
             own[tile(FIXED + j), :] = f
             if j > 0:
                 far[tile(SENT_FIXED + j - 1), :] = f
-            if j < 3:
-                near[tile(SENT_FIXED + j), :] = f
 
     lanes = {j: by_lanes(j) for j in range(ROWS) if BY_LANES[j]}
     for j in range(ROWS):
@@ -148,11 +144,19 @@
                 value = lanes[j][d]
                 if BY_LANES[j] < SUPPORT:
                     value = value + own[at, :]
-                for out in (own, near, far):
+                for out in (own, far):
                     out[at, :] = value
     for load in loads[:4]:
         load.wait()
     pack()
+
+
+def near_block(own, near):
+    near[: STORE * SUB, :] = own[: STORE * SUB, :]
+    for l in range(LAYERS):
+        rows = pl.ds((STORE + l * ROWS) * SUB, 3 * SUB)
+        near[pl.ds((STORE + l * 3) * SUB, 3 * SUB), :] = own[rows, :]
+    near[SENT_FIXED * SUB :, :] = own[FIXED * SUB : (FIXED + 3) * SUB, :]
 
 
 def well_source(wells_hbm, rates_hbm, out, wells, rates, sem):
@@ -439,15 +443,14 @@
         for x in (logk, head0, storage, fixed, support, kweight, table)
     ]
     count = lax.axis_size("space")
-    own, near, far = pl.pallas_call(
+    own, far = pl.pallas_call(
         gather_pack,
         out_shape=(
             pltpu.VMEM((FULL * SUB, LANE), f32),
-            pltpu.VMEM((NEAR * SUB, LANE), f32),
             pltpu.VMEM((FAR * SUB, LANE), f32),
         ),
         in_specs=[hbm] * 7,
-        out_specs=(vmem,) * 3,
+        out_specs=(vmem,) * 2,
         scratch_shapes=[pltpu.VMEM(x.shape, x.dtype) for x in inputs]
         + [pltpu.SemaphoreType.DMA((7,))],
         compiler_params=pltpu.CompilerParams(vmem_limit_bytes=VMEM_BYTES),
@@ -458,6 +461,14 @@
         "space",
         [(i, i + 1 if i % 2 else i - 1) for i in range(1, count - 1)],
     )
+    near = pl.pallas_call(
+        near_block,
+        out_shape=pltpu.VMEM((NEAR * SUB, LANE), f32),
+        in_specs=[vmem],
+        out_specs=vmem,
+        compiler_params=pltpu.CompilerParams(vmem_limit_bytes=VMEM_BYTES),
+        name="near_block",
+    )(own)
     near = lax.ppermute(near, "space", [(i, i ^ 1) for i in range(count)])
     src = pl.pallas_call(
         well_source,

time: 16.9 us -> 16.8 us (level)
  transfers between devices with their start and end apart: 2 -> 2, of which waited for: 1 -> 1; matrix products, arithmetic and copies ran while one was open for 0% -> 0% of each run, Pallas kernels for 14% -> 15%
where the time goes in v6:
time: 16.8 us; the launch traced here: 16.6 us
  starting transfers between devices  9.46 us (56%)
  Pallas kernels  6.08 us (36%)
  between operations  0.68 us (4%)
  waiting for transfers between devices  0.4 us (2%)
    ppermute x1, starting transfers between devices, local(): lax.ppermute(far, 'space', [(i, i + 1 if i % 2 else i - 1) for i in range...  6.21 us
    ppermute x1, starting transfers between devices, local(): near = lax.ppermute(near, 'space', [(i, i ^ 1) for i in range(count)])  3.25 us
    pallas_call x1, Pallas kernels, local(): pl.pallas_call(gather_pack, out_shape=(pltpu.VMEM((FULL * SUB, LANE), f32...  1.93 us
    pallas_call x1, Pallas kernels, local(): pl.pallas_call(after_far, out_shape=(pltpu.HBM((LAYERS, SUB * ROWS, LANE)...  1.74 us
    pallas_call x1, Pallas kernels, local(): pl.pallas_call(well_source, out_shape=pltpu.VMEM((LAYERS * 10 * SUB, LANE...  1.27 us
    pallas_call x1, Pallas kernels, local(): pl.pallas_call(before_far, out_shape=pltpu.VMEM((STATE * SUB, LANE), f32)...  1.13 us
    ppermute x1, waiting for transfers between devices, local(): lax.ppermute(far, 'space', [(i, i + 1 if i % 2 else i - 1) for i in range...  0.4 us
  transfers between devices with their start and end apart: 2, of which 1 were waited for; matrix products, arithmetic and copies ran while one was open for 0% of the time, Pallas kernels for 15%

profile of v6, /device:TPU:1, one launch (start us, length us, event | category | flops | bytes accessed | tf_op | source)
XLA Modules:
  0.0 16.6 jit_solution(14165887920752564238)
XLA Ops:
  0.6 1.9 %gather_pack.1 = (f32[544,128]{1,0:T(8,128)S(1)}, f32[512,128]{1,0:T(8,128)S(1)}) custom-call(f32[4,32,128]{2,1,0:T(8,128)} %bitcast.47, f32[4,32,128]{2,1,0:T(8,128)} %bitcast.48, f32[4,32,128]{2,1,0:T(8,128)} %bitcast.49, s32[32,128]{1,0:T(8,128)} %bitcast.53, s32[4,32,128]{2,1,0:T(8,128)} %bitcast.50, f32[4,32,128]{2,1,0:T(8,128)} %bitcast.51, ...), custom_call_target="tpu_custom_call" | custom-call | tf_op jit(solution)/shard_map/gather_pack/pallas_call | solution.py:446
  2.6 6.2 %collective-permute-start = (f32[512,128]{1,0:T(8,128)S(1)}, f32[512,128]{1,0:T(8,128)S(1)}, u32[]{:S(2)}, u32[]{:S(2)}) collective-permute-start(f32[512,128]{1,0:T(8,128)S(1)} %get-tuple-element.7), channel_id=1, source_target_pairs={{1,2},{2,1},{3,4},{4,3},{5,6},{6,5},{7,8},{8,7},{9,10},{10,9},{11,... | collective-permute-start | bytes 786440 | tf_op jit(solution)/shard_map/ppermute | solution.py:459
  8.8 3.3 %collective-permute-start.1 = (f32[504,128]{1,0:T(8,128)S(1)}, f32[504,128]{1,0:T(8,128)S(1)}, u32[]{:S(2)}, u32[]{:S(2)}) collective-permute-start(f32[504,128]{1,0:T(8,128)S(1)} %near_block.1), channel_id=1, source_target_pairs={{0,1},{1,0},{2,3},{3,2},{4,5},{5,4},{6,7},{7,6},{8,9},{9,8},{10,11... | collective-permute-start | bytes 774152 | tf_op jit(solution)/shard_map/ppermute | solution.py:472
  12.1 1.3 %well_source.1.src = f32[320,128]{1,0:T(8,128)S(1)} custom-call(s32[1,1024]{1,0:T(1,128)} %bitcast.54, f32[1,1024]{1,0:T(1,128)} %bitcast.55), custom_call_target="tpu_custom_call" | custom-call | tf_op jit(solution)/shard_map/well_source/pallas_call | solution.py:473
  13.4 0.0 collective-permute-done.1.near
  13.4 1.1 %before_far.1.st_in = f32[12288,128]{1,0:T(8,128)S(1)} custom-call(f32[544,128]{1,0:T(8,128)S(1)} %get-tuple-element.6.own, f32[504,128]{1,0:T(8,128)S(1)} %collective-permute-done.1.near, f32[320,128]{1,0:T(8,128)S(1)} %well_source.1.src), custom_call_target="tpu_custom_call" | custom-call | tf_op jit(solution)/shard_map/before_far/pallas_call | solution.py:486
  14.5 0.4 %collective-permute-done.far = f32[512,128]{1,0:T(8,128)S(1)} collective-permute-done((f32[512,128]{1,0:T(8,128)S(1)}, f32[512,128]{1,0:T(8,128)S(1)}, u32[]{:S(2)}, u32[]{:S(2)}) %collective-permute-start) | collective-permute-done | bytes 262176 | tf_op jit(solution)/shard_map/ppermute | solution.py:459
  14.9 1.7 %after_far.1 = (f32[4,32,128]{2,1,0:T(8,128)}, f32[4,4,32,128]{3,2,1,0:T(8,128)}, f32[12288,128]{1,0:T(8,128)S(1)}) custom-call(f32[544,128]{1,0:T(8,128)S(1)} %get-tuple-element.6.own, f32[512,128]{1,0:T(8,128)S(1)} %collective-permute-done.far, f32[320,128]{1,0:T(8,128)S(1)} %well_source.1.src, ...), custom_call_target="tpu_custom_call", output_to_operand_aliasing={{2}: (3, {})} | custom-call | tf_op jit(solution)/shard_map/after_far/pallas_call | solution.py:495
  (1 shorter events, 0.0 us)
Async XLA Ops:
  2.6 12.3 %collective-permute-start = (f32[512,128]{1,0:T(8,128)S(1)}, f32[512,128]{1,0:T(8,128)S(1)}, u32[]{:S(2)}, u32[]{:S(2)}) collective-permute-start(f32[512,128]{1,0:T(8,128)S(1)} %get-tuple-element.7), channel_id=1, source_target_pairs={{1,2},{2,1},{3,4},{4,3},{5,6},{6,5},{7,8},{8,7},{9,10},{10,9},{11,... | collective-permute-start | bytes 786440 | tf_op jit(solution)/shard_map/ppermute | solution.py:459
  8.8 4.5 %collective-permute-start.1 = (f32[504,128]{1,0:T(8,128)S(1)}, f32[504,128]{1,0:T(8,128)S(1)}, u32[]{:S(2)}, u32[]{:S(2)}) collective-permute-start(f32[504,128]{1,0:T(8,128)S(1)} %near_block.1), channel_id=1, source_target_pairs={{0,1},{1,0},{2,3},{3,2},{4,5},{5,4},{6,7},{7,6},{8,9},{9,8},{10,11... | collective-permute-start | bytes 774152 | tf_op jit(solution)/shard_map/ppermute | solution.py:472
